TPU v7x, 32 devices: a whole 2x2x4 slice. The times are simulated.
32 devices in a mesh: dp: 4 (over z), shard: 8 (over y, x, core).
Axes of the slice: x: 2, y: 2, z: 4, core: 2. Of those that a mesh axis runs over, the one named last changes fastest.
Arguments:
- tokens: bfloat16 [1024, 4096], P(('dp', 'shard')), may hold values from -6 to 6
- cotangent: bfloat16 [1024, 4096], P(('dp', 'shard')), may hold values from -6 to 6
- w_up: bfloat16 [4096, 14336], P('shard', 'dp'), may hold values from -0.09375 to 0.09375
- w_down: bfloat16 [14336, 4096], P('dp', 'shard'), may hold values from -0.046875 to 0.046875
- delta: float32 [128, 128, 128], P(('dp', 'shard')), may hold values from -0.5 to 0.5
- first_moment: float32 [128, 128, 128], P(('dp', 'shard')), may hold values from -1.8 to 1.8
- second_moment: float32 [128, 128, 128], P(('dp', 'shard')), may hold values from 0.02 to 0.3
- blk_row: int32 [128], replicated, may hold values from 0 to 31
- blk_col: int32 [128], replicated, may hold values from 0 to 111, as said below
- live: int32 [128], replicated, may hold values from 0 to 1, as said below
Outputs:
- layer_out: bfloat16 [1024, 4096], P(('dp', 'shard'))
- new_delta: float32 [128, 128, 128], P(('dp', 'shard'))
- new_first: float32 [128, 128, 128], P(('dp', 'shard'))
- new_second: float32 [128, 128, 128], P(('dp', 'shard'))
Inputs may be any that keep to these rules, and one draw needn't show every extreme that they name: `blk_col`: slots j to j + 8 * 4 - 1 with j a multiple of 32 name distinct blocks, all with block columns from (j // 32) * 28 to that plus 28 - 1. The live slots of each device come first among its 4 slots; some device has all 4 live.
All inputs are finite; a program needn't handle non-finite values.
Results may differ from a plain program's by a relative error of at most 0.014.
Values may be sent and summed in bfloat16 or wider, within the bound.
A program may use at most 192 MiB of HBM per device.

v0:
```python
import math

import jax
import jax.numpy as jnp
from jax import lax
from jax.sharding import PartitionSpec as P


def on_device(
    tokens, cotangent, w_up, w_down, delta, first_moment, second_moment, blk_row, blk_col, live
):
    shards = lax.axis_size("shard")
    own_slots = delta.shape[0]
    side = delta.shape[1]
    gathered_x, gathered_d = (
        lax.all_gather(tokens, "dp", axis=0, tiled=True),
        lax.all_gather(cotangent, "dp", axis=0, tiled=True),
    )
    rows = gathered_x.shape[0]
    width = gathered_x.shape[1]
    local_ff = w_up.shape[1]
    col_count = local_ff // side
    row_count = width // side
    group_index = lax.axis_index("dp")
    group_size = shards * own_slots
    begin = group_index * group_size
    slot_row = lax.dynamic_slice_in_dim(blk_row, begin, group_size)
    slot_col = lax.dynamic_slice_in_dim(blk_col, begin, group_size) - group_index * col_count
    slot_live = lax.dynamic_slice_in_dim(live, begin, group_size).astype(jnp.float32)
    row_onehot = (slot_row[:, None] == jnp.arange(row_count)[None, :]).astype(jnp.float32)
    col_onehot = (slot_col[:, None] == jnp.arange(col_count)[None, :]).astype(
        jnp.float32
    ) * slot_live[:, None]
    blocks = lax.all_gather(delta.astype(jnp.bfloat16), "shard", axis=0, tiled=True)
    pre = jnp.dot(
        gathered_x,
        lax.all_gather(w_up, "shard", axis=0, tiled=True),
        preferred_element_type=jnp.float32,
    )
    x_blocks = gathered_x.reshape(rows, row_count, side)
    picked = jnp.einsum(
        "rkb,sk->srb", x_blocks, row_onehot.astype(jnp.bfloat16), preferred_element_type=jnp.float32
    ).astype(jnp.bfloat16)
    contrib = jnp.einsum("srb,sbn->srn", picked, blocks, preferred_element_type=jnp.float32)
    placed = jnp.einsum("srn,sc->rcn", contrib, col_onehot, precision=lax.Precision.HIGHEST)
    pre = pre + placed.reshape(rows, local_ff)
    hidden = jax.nn.silu(pre).astype(jnp.bfloat16)
    down_full = lax.all_gather(w_down, "shard", axis=1, tiled=True)
    partial_out = jnp.dot(hidden, down_full, preferred_element_type=jnp.float32)
    layer_out = lax.psum_scatter(
        partial_out.astype(jnp.bfloat16), "dp", scatter_dimension=0, tiled=True
    )
    back = lax.dot_general(
        gathered_d, down_full, (((1,), (1,)), ((), ())), preferred_element_type=jnp.float32
    )
    sigma = jax.nn.sigmoid(pre)
    dpre = (back * sigma * (1.0 + pre * (1.0 - sigma))).astype(jnp.bfloat16)
    factor = 1.0 / math.sqrt(rows * shards)
    slope_blocks = dpre.reshape(rows, col_count, side)
    chosen = jnp.einsum(
        "rcb,sc->srb",
        slope_blocks,
        col_onehot.astype(jnp.bfloat16),
        preferred_element_type=jnp.float32,
    ).astype(jnp.bfloat16)
    grads = jnp.einsum("srk,srn->skn", picked, chosen, preferred_element_type=jnp.float32)
    grads = grads * factor
    owned_grad = lax.psum_scatter(
        grads.astype(jnp.bfloat16), "shard", scatter_dimension=0, tiled=True
    ).astype(jnp.float32)
    new_first = 0.9 * first_moment + 0.1 * owned_grad
    new_second = 0.95 * second_moment + 0.05 * owned_grad * owned_grad
    corrected_first = new_first / (1.0 - 0.9**10)
    corrected_second = new_second / (1.0 - 0.95**10)
    new_delta = delta - 0.01 * corrected_first / (jnp.sqrt(corrected_second) + 1e-08)
    return (layer_out, new_delta, new_first, new_second)


def solution(mesh):
    in_specs = (
        P(("dp", "shard"), None),
        P(("dp", "shard"), None),
        P("shard", "dp"),
        P("dp", "shard"),
        P(("dp", "shard"), None, None),
        P(("dp", "shard"), None, None),
        P(("dp", "shard"), None, None),
        P(),
        P(),
        P(),
    )
    out_specs = (
        P(("dp", "shard"), None),
        P(("dp", "shard"), None, None),
        P(("dp", "shard"), None, None),
        P(("dp", "shard"), None, None),
    )
    return jax.shard_map(
        on_device, mesh=mesh, in_specs=in_specs, out_specs=out_specs, check_vma=False
    )
```

profile of v0, /device:TPU:0, one launch (start us, length us, event | category | flops | bytes accessed | tf_op | source)
XLA Modules:
  0.0 483.0 jit_solution(6371794799208030536)
XLA Ops:
  7.2 0.0 all-gather.6.cloned.1.call-start
  7.2 0.7 all-gather.6.cloned.1.call-update
  7.9 0.0 all-gather.10.cloned.1.call-start
  7.9 1.6 convert_element_type.41
  9.6 0.0 all-gather.10.cloned.1.call-update
  9.6 0.0 all-gather.8.cloned.1.call-start
  9.6 0.7 all-gather.8.cloned.1.call-update
  10.3 0.0 copy-start.6
  10.3 0.0 copy-start.4
  10.4 0.0 copy-start.5
  10.4 0.0 all-gather.14.cloned.1.call-start
  10.4 0.5 all-gather.14.cloned.1.call-update
  10.9 0.0 all-gather.12.cloned.1.call-start
  11.0 0.5 all-gather.12.cloned.1.call-update
  11.5 0.0 reduce-scatter.5.cloned.1.call-start
  11.6 0.0 copy-done.6
  11.6 0.1 dynamic_slice.11
  11.7 0.0 copy-done.4
  11.7 0.1 dynamic-slice_convert_fusion
  11.8 28.5 %all-gather.6.cloned.1.call-done = bf16[128,4096]{1,0:T(8,128)(2,1)} async-done(((bf16[32,4096]{1,0:T(8,128)(2,1)}), bf16[128,4096]{1,0:T(8,128)(2,1)}) %all-gather.6.cloned.1.call-update) | async-done | bytes 1048592 | tf_op jit(solution)/shard_map/all_gather | solution.py:16
  40.2 1.4 copy.30
  41.7 0.5 convolution_convert_fusion.2
  42.2 1.0 copy.26
  43.2 22.6 %all-gather.10.cloned.1.call-done = bf16[32,128,128]{2,1,0:T(8,128)(2,1)} async-done(((bf16[4,128,128]{2,1,0:T(8,128)(2,1)}), bf16[32,128,128]{2,1,0:T(8,128)(2,1)}) %all-gather.10.cloned.1.call-update) | async-done | bytes 1048592 | tf_op jit(solution)/shard_map/all_gather | solution.py:34
  65.7 1.7 fusion.27
  67.5 3.0 fusion.4
  70.5 1.8 copy.22
  72.3 1.8 copy.23
  74.2 136.5 %all-gather.8.cloned.1.call-done = bf16[4096,3584]{1,0:T(8,128)(2,1)} async-done(((bf16[512,3584]{1,0:T(8,128)(2,1)}), bf16[4096,3584]{1,0:T(8,128)(2,1)}) %all-gather.8.cloned.1.call-update) | async-done | bytes 29360144 | tf_op jit(solution)/shard_map/all_gather | solution.py:37
  210.7 15.1 %convolution_add_fusion = f32[128,3584]{1,0:T(8,128)} fusion(f32[128,3584]{1,0:T(8,128)S(1)} %copy.23, bf16[128,4096]{1,0:T(8,128)(2,1)} %all-gather.6.cloned.1.call-done, bf16[4096,3584]{1,0:T(8,128)(2,1)} %all-gather.8.cloned.1.call-done), kind=kOutput, calls=%fused_computation.2 | convolution fusion | flops 3758555136 | bytes 34078720 | tf_op jit(solution)/shard_map/dot_general | solution.py:35
  225.8 14.3 %all-gather.14.cloned.1.call-done = bf16[128,4096]{1,0:T(8,128)(2,1)} async-done(((bf16[32,4096]{1,0:T(8,128)(2,1)}), bf16[128,4096]{1,0:T(8,128)(2,1)}) %all-gather.14.cloned.1.call-update) | async-done | bytes 1048592 | tf_op jit(solution)/shard_map/all_gather | solution.py:17
  240.1 150.1 %all-gather.12.cloned.1.call-done = bf16[3584,4096]{1,0:T(8,128)(2,1)} async-done(((bf16[3584,512]{1,0:T(8,128)(2,1)}), bf16[3584,4096]{1,0:T(8,128)(2,1)}) %all-gather.12.cloned.1.call-update) | async-done | bytes 29360144 | tf_op jit(solution)/shard_map/all_gather | solution.py:48
  390.2 15.4 %fusion.1 = bf16[128,3584]{1,0:T(8,128)(2,1)S(1)} fusion(bf16[128,4096]{1,0:T(8,128)(2,1)} %all-gather.14.cloned.1.call-done, bf16[3584,4096]{1,0:T(8,128)(2,1)} %all-gather.12.cloned.1.call-done, f32[128,3584]{1,0:T(8,128)} %convolution_add_fusion), kind=kOutput, calls=%fused_computation.3 | convolution fusion | flops 3762225152 | bytes 33161216 | tf_op jit(solution)/shard_map/dot_general | solution.py:53
  405.6 0.6 copy.24
  406.2 1.3 copy.25
  407.5 0.5 convolution_convert_fusion.1
  408.0 1.9 multiply_convert_fusion
  409.9 0.0 reduce-scatter.5.cloned.1.call-update
  409.9 0.0 copy-start.1
  409.9 0.0 copy-start.2
  409.9 0.0 copy-start.3
  409.9 0.0 reduce-scatter.3.cloned.1.call-start
  410.0 0.0 copy-done
  410.0 14.8 %convolution_convert_fusion = bf16[128,4096]{1,0:T(8,128)(2,1)} fusion(bf16[3584,4096]{1,0:T(8,128)(2,1)} %all-gather.12.cloned.1.call-done, f32[128,3584]{1,0:T(8,128)S(1)} %copy-done), kind=kOutput, calls=%fused_computation.4 | convolution fusion | flops 3760914432 | bytes 32243712 | tf_op jit(solution)/shard_map/dot_general | solution.py:49
  424.8 0.0 reduce-scatter.3.cloned.1.call-update
  424.8 21.3 %reduce-scatter.5.cloned.1.call-done = bf16[4,128,128]{2,1,0:T(8,128)(2,1)} async-done(((bf16[32,128,128]{2,1,0:T(8,128)(2,1)}), bf16[4,128,128]{2,1,0:T(8,128)(2,1)}) %reduce-scatter.5.cloned.1.call-update) | async-done | bytes 131088 | tf_op jit(solution)/shard_map/reduce_scatter | solution.py:68
  446.1 1.9 divide_subtract_fusion
  448.0 28.2 %reduce-scatter.3.cloned.1.call-done = bf16[32,4096]{1,0:T(8,128)(2,1)} async-done(((bf16[128,4096]{1,0:T(8,128)(2,1)}), bf16[32,4096]{1,0:T(8,128)(2,1)}) %reduce-scatter.3.cloned.1.call-update) | async-done | bytes 262160 | tf_op jit(solution)/shard_map/reduce_scatter | solution.py:50
  (5 shorter events, 0.0 us)
Async XLA Ops:
  7.2 33.1 %all-gather.6.cloned.1.call-start = ((), (), s32[]{:S(2)}) async-start(), calls=%async_computation.2 | async-start | bytes 1310720 | tf_op jit(solution)/shard_map/all_gather | solution.py:16
  7.9 57.8 %all-gather.10.cloned.1.call-start = ((), (), s32[]{:S(2)}) async-start(), calls=%async_computation.4 | async-start | bytes 1179648 | tf_op jit(solution)/shard_map/all_gather | solution.py:34
  9.6 201.1 %all-gather.8.cloned.1.call-start = ((), (), s32[]{:S(2)}) async-start(), calls=%async_computation.3 | async-start | bytes 33030144 | tf_op jit(solution)/shard_map/all_gather | solution.py:37
  10.3 1.3 copy-start.6
  10.3 1.3 copy-start.4
  10.4 1.3 copy-start.5
  10.4 229.7 %all-gather.14.cloned.1.call-start = ((), (), s32[]{:S(2)}) async-start(), calls=%async_computation.7 | async-start | bytes 1310720 | tf_op jit(solution)/shard_map/all_gather | solution.py:17
  10.9 379.2 %all-gather.12.cloned.1.call-start = ((), (), s32[]{:S(2)}) async-start(), calls=%async_computation.5 | async-start | bytes 33030144 | tf_op jit(solution)/shard_map/all_gather | solution.py:48
  11.5 434.5 %reduce-scatter.5.cloned.1.call-start = ((), (), s32[]{:S(2)}) async-start(), calls=%async_computation.8 | async-start | bytes 1179648 | tf_op jit(solution)/shard_map/reduce_scatter | solution.py:68
  408.0 2.0 copy-start
  409.9 36.2 %copy-start.1 = (f32[4,128,128]{2,1,0:T(8,128)S(1)}, f32[4,128,128]{2,1,0:T(8,128)}, u32[]{:S(2)}) copy-start(f32[4,128,128]{2,1,0:T(8,128)} %param.14) | copy-start | bytes 786436
  409.9 36.2 %copy-start.2 = (f32[4,128,128]{2,1,0:T(8,128)S(1)}, f32[4,128,128]{2,1,0:T(8,128)}, u32[]{:S(2)}) copy-start(f32[4,128,128]{2,1,0:T(8,128)} %param.15) | copy-start | bytes 786436
  409.9 36.2 %copy-start.3 = (f32[4,128,128]{2,1,0:T(8,128)S(1)}, f32[4,128,128]{2,1,0:T(8,128)}, u32[]{:S(2)}) copy-start(f32[4,128,128]{2,1,0:T(8,128)} %param.16) | copy-start | bytes 786436
  409.9 66.2 %reduce-scatter.3.cloned.1.call-start = ((), (), s32[]{:S(2)}) async-start(), calls=%async_computation.6 | async-start | bytes 1310720 | tf_op jit(solution)/shard_map/reduce_scatter | solution.py:50
Sparse Core Ops, SparseCore 0:
  9.6 30.6 all-gather.5
  42.7 22.9 all-gather.9
  67.6 143.0 all-gather.7
  212.1 27.9 all-gather.13
  241.8 148.3 all-gather.11
  410.0 36.0 reduce-scatter.4
  448.9 27.1 reduce-scatter.2
where the time goes:
time: 483 us
  waiting for transfers between devices  404 us (84%)
  matrix products  52.9 us (11%)
  between operations  14.3 us (3%)
  local copies, waits for them, and re-layouts  8.1 us (2%)
    all_gather x1, waiting for transfers between devices, on_device(): down_full = lax.all_gather(w_down, 'shard', axis=1, tiled=True)  150 us
    all_gather x1, waiting for transfers between devices, on_device(): lax.all_gather(w_up, 'shard', axis=0, tiled=True)  137 us
    all_gather x1, waiting for transfers between devices, on_device(): lax.all_gather(tokens, 'dp', axis=0, tiled=True)  28.5 us
    reduce_scatter x1, waiting for transfers between devices, on_device(): lax.psum_scatter(partial_out.astype(jnp.bfloat16), 'dp', scatter_dimensio...  28.2 us
    all_gather x1, waiting for transfers between devices, on_device(): lax.all_gather(delta.astype(jnp.bfloat16), 'shard', axis=0, tiled=True)  22.6 us
    reduce_scatter x1, waiting for transfers between devices, on_device(): lax.psum_scatter(grads.astype(jnp.bfloat16), 'shard', scatter_dimension=0...  21.3 us
    dot_general x1, matrix products, on_device(): lax.dot_general(gathered_d, down_full, (((1,), (1,)), ((), ())), preferre...  15.4 us
    dot_general x1, matrix products, on_device(): jnp.dot(gathered_x, lax.all_gather(w_up, 'shard', axis=0, tiled=True), pr...  15.1 us
  transfers between devices with their start and end apart: 7, of which 7 were waited for; matrix products, arithmetic and copies ran while one was open for 9% of the time, Pallas kernels for 0%

commit v1 on v0

--- a/solution.py
+++ b/solution.py
@@ -32,11 +32,14 @@
         jnp.float32
     ) * slot_live[:, None]
     blocks = lax.all_gather(delta.astype(jnp.bfloat16), "shard", axis=0, tiled=True)
-    pre = jnp.dot(
-        gathered_x,
-        lax.all_gather(w_up, "shard", axis=0, tiled=True),
-        preferred_element_type=jnp.float32,
-    )
+    x_cols = lax.all_to_all(gathered_x, "shard", split_axis=1, concat_axis=0, tiled=True)
+    d_cols = lax.all_to_all(gathered_d, "shard", split_axis=1, concat_axis=0, tiled=True)
+    pre_part = jnp.dot(x_cols, w_up, preferred_element_type=jnp.float32).astype(jnp.bfloat16)
+    pre = lax.psum_scatter(pre_part, "shard", scatter_dimension=0, tiled=True).astype(jnp.float32)
+    back_part = lax.dot_general(
+        d_cols, w_down, (((1,), (1,)), ((), ())), preferred_element_type=jnp.float32
+    ).astype(jnp.bfloat16)
+    back = lax.psum_scatter(back_part, "shard", scatter_dimension=0, tiled=True).astype(jnp.float32)
     x_blocks = gathered_x.reshape(rows, row_count, side)
     picked = jnp.einsum(
         "rkb,sk->srb", x_blocks, row_onehot.astype(jnp.bfloat16), preferred_element_type=jnp.float32
@@ -45,14 +48,12 @@
     placed = jnp.einsum("srn,sc->rcn", contrib, col_onehot, precision=lax.Precision.HIGHEST)
     pre = pre + placed.reshape(rows, local_ff)
     hidden = jax.nn.silu(pre).astype(jnp.bfloat16)
-    down_full = lax.all_gather(w_down, "shard", axis=1, tiled=True)
-    partial_out = jnp.dot(hidden, down_full, preferred_element_type=jnp.float32)
-    layer_out = lax.psum_scatter(
-        partial_out.astype(jnp.bfloat16), "dp", scatter_dimension=0, tiled=True
-    )
-    back = lax.dot_general(
-        gathered_d, down_full, (((1,), (1,)), ((), ())), preferred_element_type=jnp.float32
-    )
+    hidden_all = lax.all_gather(hidden, "shard", axis=0, tiled=True)
+    partial_out = jnp.dot(hidden_all, w_down, preferred_element_type=jnp.float32)
+    partial_out = partial_out.astype(jnp.bfloat16).reshape(shards, lax.axis_size("dp"), -1, w_down.shape[1])
+    partial_out = partial_out.transpose(1, 0, 2, 3).reshape(-1, w_down.shape[1])
+    out_cols = lax.psum_scatter(partial_out, "dp", scatter_dimension=0, tiled=True)
+    layer_out = lax.all_to_all(out_cols, "shard", split_axis=0, concat_axis=1, tiled=True)
     sigma = jax.nn.sigmoid(pre)
     dpre = (back * sigma * (1.0 + pre * (1.0 - sigma))).astype(jnp.bfloat16)
     factor = 1.0 / math.sqrt(rows * shards)

time: 483 us -> 377 us (0.78)
  waiting for transfers between devices: 404 us -> 266 us
  blocking collectives: 0 us -> 38.9 us
  matrix products: 52.9 us -> 31.8 us
  local copies, waits for them, and re-layouts: 8.1 us -> 14.5 us
    all_gather x2 -> x1, waiting for transfers between devices: 287 us -> 49.9 us  [on_device(): hidden_all = lax.all_gather(hidden, 'shard', axis=0, tiled=True)]
    reduce_scatter x1 -> x3, waiting for transfers between devices: 28.2 us -> 150 us  [the longest x1 70.5 us: on_device(): lax.psum_scatter(back_part, 'shard', scatter_dimension=0, tiled=True)]
    all_to_all x0 -> x2, blocking collectives: none -> 38.9 us  [the longest x1 20.1 us: on_device(): lax.all_to_all(gathered_d, 'shard', split_axis=1, concat_axis=0, tiled=True)]
    all_gather x1, waiting for transfers between devices: 22.6 us -> 0.02 us  [on_device(): lax.all_gather(delta.astype(jnp.bfloat16), 'shard', axis=0, tiled=True)]
    dot_general x3, matrix products: 45.3 us -> 24.3 us  [the longest x1 8.19 us: on_device(): lax.dot_general(d_cols, w_down, (((1,), (1,)), ((), ())), preferred_eleme...]
    all_gather x1, waiting for transfers between devices: 14.3 us -> 0.02 us  [on_device(): lax.all_gather(cotangent, 'dp', axis=0, tiled=True)]
    reduce_scatter x1, waiting for transfers between devices: 21.3 us -> 34.5 us  [on_device(): lax.psum_scatter(grads.astype(jnp.bfloat16), 'shard', scatter_dimension=0...]
  transfers between devices with their start and end apart: 7 -> 9, of which waited for: 7 -> 6; matrix products, arithmetic and copies ran while one was open for 9% -> 10% of each run, Pallas kernels for 0% -> 0%
where the time goes in v1:
time: 377 us
  waiting for transfers between devices  266 us (71%)
  blocking collectives  38.9 us (10%)
  matrix products  31.8 us (8%)
  local copies, waits for them, and re-layouts  14.5 us (4%)
  between operations  14.3 us (4%)
  other arithmetic  7.16 us (2%)
  starting transfers between devices  4.16 us (1%)
    reduce_scatter x1, waiting for transfers between devices, on_device(): lax.psum_scatter(back_part, 'shard', scatter_dimension=0, tiled=True)  70.5 us
    reduce_scatter x1, waiting for transfers between devices, on_device(): lax.psum_scatter(pre_part, 'shard', scatter_dimension=0, tiled=True)  56.5 us
    all_gather x1, waiting for transfers between devices, on_device(): hidden_all = lax.all_gather(hidden, 'shard', axis=0, tiled=True)  49.9 us
    reduce_scatter x1, waiting for transfers between devices, on_device(): lax.psum_scatter(grads.astype(jnp.bfloat16), 'shard', scatter_dimension=0...  34.5 us
    all_gather x1, waiting for transfers between devices, on_device(): lax.all_gather(tokens, 'dp', axis=0, tiled=True)  29.8 us
    reduce_scatter x1, waiting for transfers between devices, on_device(): lax.psum_scatter(partial_out, 'dp', scatter_dimension=0, tiled=True)  22.8 us
    all_to_all x1, blocking collectives, on_device(): lax.all_to_all(gathered_d, 'shard', split_axis=1, concat_axis=0, tiled=True)  20.1 us
    all_to_all x1, blocking collectives, on_device(): lax.all_to_all(gathered_x, 'shard', split_axis=1, concat_axis=0, tiled=True)  18.8 us
  transfers between devices with their start and end apart: 9, of which 6 were waited for; matrix products, arithmetic and copies ran while one was open for 10% of the time, Pallas kernels for 0%

profile of v1, /device:TPU:0, one launch (start us, length us, event | category | flops | bytes accessed | tf_op | source)
XLA Modules:
  0.0 376.5 jit_solution(14674732388146369441)
XLA Ops:
  7.2 0.0 all-gather.5.cloned.1.call-start
  7.2 0.7 all-gather.5.cloned.1.call-update
  7.9 0.0 all-gather.11.cloned.1.call-start
  7.9 0.7 all-gather.11.cloned.1.call-update
  8.6 0.0 all-gather.7.cloned.1.call-start
  8.7 1.6 convert_element_type.55
  10.3 0.0 reduce-scatter.5.cloned.1.call-start
  10.4 29.8 %all-gather.5.cloned.1.call-done = bf16[128,4096]{1,0:T(8,128)(2,1)} async-done(((bf16[32,4096]{1,0:T(8,128)(2,1)}), bf16[128,4096]{1,0:T(8,128)(2,1)}) %all-gather.5.cloned.1.call-update) | async-done | bytes 1048592 | tf_op jit(solution)/shard_map/all_gather | solution.py:16
  40.2 1.6 copy.36
  41.9 18.8 %all_to_all.57 = bf16[128,8,512]{0,2,1:T(8,128)(2,1)S(1)} all-to-all(bf16[128,8,512]{0,2,1:T(8,128)(2,1)S(1)} %bitcast.47), channel_id=1, replica_groups=mesh['dp'=4,'shard'=8] {'shard'}, dimensions={1} | all-to-all | bytes 2097152 | tf_op jit(solution)/shard_map/all_to_all | solution.py:35
  60.7 0.5 copy.37
  61.2 8.1 %convolution_convert_fusion.1 = bf16[1024,3584]{1,0:T(8,128)(2,1)} fusion(bf16[1024,512]{1,0:T(8,128)(2,1)S(1)} %bitcast.49, bf16[512,3584]{1,0:T(8,128)(2,1)} %param.12), kind=kOutput, calls=%fused_computation.1 | convolution fusion | flops 3761766400 | bytes 12058624 | tf_op jit(solution)/shard_map/dot_general | solution.py:37
  69.3 0.0 reduce-scatter.9.cloned.1.call-start
  69.4 1.6 copy.45
  71.0 20.1 %all_to_all.58 = bf16[128,8,512]{0,2,1:T(8,128)(2,1)S(1)} all-to-all(bf16[128,8,512]{0,2,1:T(8,128)(2,1)S(1)} %bitcast.45), channel_id=1, replica_groups=mesh['dp'=4,'shard'=8] {'shard'}, dimensions={1} | all-to-all | bytes 2097152 | tf_op jit(solution)/shard_map/all_to_all | solution.py:36
  91.1 0.5 copy.46
  91.6 8.2 %convolution_convert_fusion = bf16[1024,3584]{1,0:T(8,128)(2,1)} fusion(bf16[1024,512]{1,0:T(8,128)(2,1)S(1)} %bitcast.50, bf16[3584,512]{1,0:T(8,128)(2,1)} %param.13), kind=kOutput, calls=%fused_computation | convolution fusion | flops 3761766400 | bytes 12058624 | tf_op jit(solution)/shard_map/dot_general | solution.py:39
  99.9 0.0 all-gather.9.cloned.1.call-start
  99.9 0.6 copy-done.7
  100.5 0.1 dynamic_slice.11
  100.6 0.1 dynamic-slice_convert_fusion
  100.6 0.5 copy-done
  101.1 0.2 copy.54
  101.3 0.5 convolution_convert_fusion.4
  101.8 1.0 copy.49
  102.8 0.0 all-gather.7.cloned.1.call-done
  102.8 1.7 fusion.23
  104.6 3.0 fusion.2
  107.6 1.8 copy.41
  109.4 2.2 copy.42
  111.6 56.5 %reduce-scatter.5.cloned.1.call-done = bf16[128,3584]{1,0:T(8,128)(2,1)} async-done(((bf16[1024,3584]{1,0:T(8,128)(2,1)}), bf16[128,3584]{1,0:T(8,128)(2,1)}) %reduce-scatter.5.cloned.1.call-update) | async-done | bytes 917520 | tf_op jit(solution)/shard_map/reduce_scatter | solution.py:38
  168.2 70.5 %reduce-scatter.9.cloned.1.call-done = bf16[128,3584]{1,0:T(8,128)(2,1)} async-done(((bf16[1024,3584]{1,0:T(8,128)(2,1)}), bf16[128,3584]{1,0:T(8,128)(2,1)}) %reduce-scatter.9.cloned.1.call-update) | async-done | bytes 917520 | tf_op jit(solution)/shard_map/reduce_scatter | solution.py:42
  238.7 3.6 multiply_convert_fusion.1
  242.3 0.2 reduce-scatter.7.cloned.1.call-start
  242.5 49.9 %all-gather.9.cloned.1.call-done = bf16[1024,3584]{1,0:T(8,128)(2,1)} async-done(((bf16[128,3584]{1,0:T(8,128)(2,1)}), bf16[1024,3584]{1,0:T(8,128)(2,1)}) %all-gather.9.cloned.1.call-update) | async-done | bytes 7340048 | tf_op jit(solution)/shard_map/all_gather | solution.py:51
  292.4 8.1 %convolution_convert_fusion.2 = bf16[1024,512]{1,0:T(8,128)(2,1)S(1)} fusion(bf16[1024,3584]{1,0:T(8,128)(2,1)} %all-gather.9.cloned.1.call-done, bf16[3584,512]{1,0:T(8,128)(2,1)} %param.13), kind=kOutput, calls=%fused_computation.10 | convolution fusion | flops 3758620672 | bytes 12058624 | tf_op jit(solution)/shard_map/dot_general | solution.py:52
  300.5 1.1 copy.43
  301.6 0.0 reduce-scatter.11.cloned.1.call-start
  301.6 0.4 copy-done.1
  302.0 0.6 copy.47
  302.6 1.1 copy.48
  303.8 0.5 convolution_convert_fusion.3
  304.3 1.8 multiply_convert_fusion
  306.1 22.8 %reduce-scatter.7.cloned.1.call-done = bf16[256,512]{1,0:T(8,128)(2,1)} async-done(((bf16[1024,512]{1,0:T(8,128)(2,1)}), bf16[256,512]{1,0:T(8,128)(2,1)}) %reduce-scatter.7.cloned.1.call-update) | async-done | bytes 262160 | tf_op jit(solution)/shard_map/reduce_scatter | solution.py:55
  328.9 3.7 all-to-all-start.1
  332.5 34.5 %reduce-scatter.11.cloned.1.call-done = bf16[4,128,128]{2,1,0:T(8,128)(2,1)} async-done(((bf16[32,128,128]{2,1,0:T(8,128)(2,1)}), bf16[4,128,128]{2,1,0:T(8,128)(2,1)}) %reduce-scatter.11.cloned.1.call-update) | async-done | bytes 131088 | tf_op jit(solution)/shard_map/reduce_scatter | solution.py:69
  367.1 1.9 divide_subtract_fusion
  368.9 0.7 copy.53
  (21 shorter events, 0.2 us)
Async XLA Ops:
  7.2 33.1 %all-gather.5.cloned.1.call-start = ((), (), s32[]{:S(2)}) async-start(), calls=%async_computation.7 | async-start | bytes 1310720 | tf_op jit(solution)/shard_map/all_gather | solution.py:16
  7.9 61.5 %all-gather.11.cloned.1.call-start = ((), (), s32[]{:S(2)}) async-start(), calls=%async_computation.12 | async-start | bytes 1310720 | tf_op jit(solution)/shard_map/all_gather | solution.py:17
  8.6 94.2 %all-gather.7.cloned.1.call-start = ((), (), s32[]{:S(2)}) async-start(), calls=%async_computation.9 | async-start | bytes 1179648 | tf_op jit(solution)/shard_map/all_gather | solution.py:34
  10.3 157.8 %reduce-scatter.5.cloned.1.call-start = ((), (), s32[]{:S(2)}) async-start(), calls=%async_computation.8 | async-start | bytes 8257536 | tf_op jit(solution)/shard_map/reduce_scatter | solution.py:38
  69.3 169.4 %reduce-scatter.9.cloned.1.call-start = ((), (), s32[]{:S(2)}) async-start(), calls=%async_computation.13 | async-start | bytes 8257536 | tf_op jit(solution)/shard_map/reduce_scatter | solution.py:42
  99.8 0.7 copy-start.7
  99.8 0.7 copy-start.5
  99.8 0.7 copy-start.6
  99.8 1.3 copy-start
  99.9 192.5 %all-gather.9.cloned.1.call-start = ((), (), s32[]{:S(2)}) async-start(), calls=%async_computation.10 | async-start | bytes 8257536 | tf_op jit(solution)/shard_map/all_gather | solution.py:51
  242.3 86.6 %reduce-scatter.7.cloned.1.call-start = ((), (), s32[]{:S(2)}) async-start(), calls=%async_computation.11 | async-start | bytes 1310720 | tf_op jit(solution)/shard_map/reduce_scatter | solution.py:55
  300.4 1.6 copy-start.1
  301.6 65.5 %reduce-scatter.11.cloned.1.call-start = ((), (), s32[]{:S(2)}) async-start(), calls=%async_computation.14 | async-start | bytes 1179648 | tf_op jit(solution)/shard_map/reduce_scatter | solution.py:69
  304.2 62.8 %copy-start.2 = (f32[4,128,128]{2,1,0:T(8,128)S(1)}, f32[4,128,128]{2,1,0:T(8,128)}, u32[]{:S(2)}) copy-start(f32[4,128,128]{2,1,0:T(8,128)} %param.14) | copy-start | bytes 786436
  304.2 62.8 %copy-start.3 = (f32[4,128,128]{2,1,0:T(8,128)S(1)}, f32[4,128,128]{2,1,0:T(8,128)}, u32[]{:S(2)}) copy-start(f32[4,128,128]{2,1,0:T(8,128)} %param.15) | copy-start | bytes 786436
  304.3 62.8 %copy-start.4 = (f32[4,128,128]{2,1,0:T(8,128)S(1)}, f32[4,128,128]{2,1,0:T(8,128)}, u32[]{:S(2)}) copy-start(f32[4,128,128]{2,1,0:T(8,128)} %param.16) | copy-start | bytes 786436
  328.9 40.1 %all-to-all-start.1 = ((bf16[8,32,512]{2,1,0:T(8,128)(2,1)}), bf16[8,32,512]{2,1,0:T(8,128)(2,1)S(1)}, u32[]{:S(2)}, u32[]{:S(2)}) async-start(bf16[8,32,512]{2,1,0:T(8,128)(2,1)} %bitcast.53), calls=%async_computation.3 | async-start | bytes 524288 | tf_op jit(solution)/shard_map/all_to_all | solution.py:56
Sparse Core Ops, SparseCore 0:
  9.6 30.6 all-gather.4
  41.8 27.4 all-gather.10
  71.7 26.1 all-gather.6
  101.2 66.9 reduce-scatter.4
  171.8 66.8 reduce-scatter.8
  242.4 49.9 all-gather.8
  301.7 27.1 reduce-scatter.6
  332.4 34.6 reduce-scatter.10

commit v2 on v1

--- a/solution.py
+++ b/solution.py
@@ -1,9 +1,218 @@
+import functools
 import math
 
 import jax
 import jax.numpy as jnp
 from jax import lax
+from jax.experimental import pallas as pl
+from jax.experimental.pallas import tpu as pltpu
 from jax.sharding import PartitionSpec as P
+
+F32 = jnp.float32
+BF16 = jnp.bfloat16
+VMEM_LIMIT = 62 * 1024 * 1024
+VMEM_PLAN = 56 * 1024 * 1024
+
+
+def flip(place, mask):
+    bit = 1
+    while bit <= mask:
+        if mask & bit:
+            place = place + bit * (1 - 2 * ((place // bit) % 2))
+        bit *= 2
+    return place
+
+
+class Tree:
+    def __init__(self, n):
+        self.n = n
+        self.bits = n.bit_length() - 1
+        rest = list(range(1, self.bits))
+        self.orders = ([0] + rest, [0] + rest[::-1])
+
+    def first(self, h, j):
+        return next(b for b in self.orders[h] if j >> b & 1)
+
+    def children(self, h, j):
+        found = []
+        for b in self.orders[h]:
+            if j >> b & 1:
+                break
+            found.append(j | 1 << b)
+        return found
+
+
+def tile_of(width):
+    tile = min(width, 1024) // 128 * 128
+    while width % tile:
+        tile -= 128
+    return tile
+
+
+def middle_kernel(
+    n, x_ref, d_ref, up_ref, down_ref, placed_ref, out_ref, dpre_ref,
+    part, got, hid, pre_s, send_s, recv_s, hsend_s, hrecv_s,
+):
+    tree = Tree(n)
+    me = lax.axis_index("shard")
+    rows = placed_ref.shape[0]
+    half = part.shape[4]
+    tile = tile_of(half)
+    tiles = half // tile
+
+    barrier = pltpu.get_barrier_semaphore()
+    for b in range(tree.bits):
+        pl.semaphore_signal(
+            barrier, inc=1, device_id={"shard": flip(me, 1 << b)}, device_id_type=pl.DeviceIdType.MESH
+        )
+    pl.semaphore_wait(barrier, tree.bits)
+
+    def sum_copy(t, h, j):
+        return pltpu.make_async_remote_copy(
+            src_ref=part.at[t, h, j],
+            dst_ref=got.at[t, h, j],
+            send_sem=send_s.at[t, h, j],
+            recv_sem=recv_s.at[t, h, j],
+            device_id={"shard": flip(me, 1 << tree.first(h, j))},
+            device_id_type=pl.DeviceIdType.MESH,
+        )
+
+    def hid_copy(h, src, dst):
+        return pltpu.make_async_remote_copy(
+            src_ref=hid.at[h, src],
+            dst_ref=hid.at[h, dst],
+            send_sem=hsend_s.at[h, dst],
+            recv_sem=hrecv_s.at[h, dst],
+            device_id={"shard": flip(me, src ^ dst)},
+            device_id_type=pl.DeviceIdType.MESH,
+        )
+
+    def chunk(t, h, j):
+        source = x_ref if t == 0 else d_ref
+        at = pl.ds(pl.multiple_of(flip(me, j) * rows, rows), rows)
+        kids = tree.children(h, j)
+        for kid in kids:
+            sum_copy(t, h, kid).wait_recv()
+
+        def body(i, _):
+            cols = pl.ds(pl.multiple_of(i * tile, 128), tile)
+            wide = pl.ds(pl.multiple_of(h * half + i * tile, 128), tile)
+            if t == 0:
+                total = jnp.dot(source[at, :], up_ref[:, wide], preferred_element_type=F32)
+            else:
+                total = lax.dot_general(
+                    source[at, :], down_ref[wide, :], (((1,), (1,)), ((), ())), preferred_element_type=F32
+                )
+            for kid in kids:
+                total = total + got[t, h, kid, :, cols].astype(F32)
+            if j:
+                part[t, h, j, :, cols] = total.astype(BF16)
+            elif t == 0:
+                pre = total + placed_ref[:, wide]
+                pre_s[h, :, cols] = pre
+                hid[h, 0, :, cols] = (pre * jax.nn.sigmoid(pre)).astype(BF16)
+            else:
+                pre = pre_s[h, :, cols]
+                sigma = jax.nn.sigmoid(pre)
+                dpre_ref[:, wide] = (total * sigma * (1.0 + pre * (1.0 - sigma))).astype(BF16)
+            return 0
+
+        lax.fori_loop(0, tiles, body, 0)
+        if j:
+            sum_copy(t, h, j).start()
+
+    def project(j):
+        at = pl.ds(pl.multiple_of(flip(me, j) * rows, rows), rows)
+        total = jnp.dot(hid[0, j], down_ref[pl.ds(0, half), :], preferred_element_type=F32)
+        total += jnp.dot(hid[1, j], down_ref[pl.ds(half, half), :], preferred_element_type=F32)
+        out_ref[at, :] = total.astype(BF16)
+
+    odd = sorted((j for j in range(n) if j & 1), key=lambda j: -j.bit_count())
+    even = [(h, j) for j in range(2, n, 2) for h in range(2)]
+    even.sort(key=lambda c: (-c[1].bit_count(), len(tree.children(*c))))
+    early = [c for c in even if len(tree.children(*c)) == 1]
+    late = [c for c in even if len(tree.children(*c)) > 1]
+    for t in range(2):
+        for j in odd:
+            for h in range(2):
+                chunk(t, h, j)
+    for h, j in even:
+        chunk(0, h, j)
+    for h, j in early:
+        chunk(1, h, j)
+    for h in range(2):
+        chunk(0, h, 0)
+        for j in sorted(tree.children(h, 0), key=lambda j: -len(tree.children(h, j))):
+            hid_copy(h, 0, j).start()
+    for h, j in late:
+        chunk(1, h, j)
+    project(0)
+    arrivals = [(h, j) for j in range(1, n) for h in range(2)]
+    arrivals.sort(key=lambda c: (c[1].bit_count(), -len(tree.children(*c))))
+    seen = [0] * n
+    ready = []
+    for at, (h, j) in enumerate(arrivals):
+        hid_copy(h, j ^ (1 << tree.first(h, j)), j).wait_recv()
+        for kid in sorted(tree.children(h, j), key=lambda k: -len(tree.children(h, k))):
+            hid_copy(h, j, kid).start()
+        seen[j] += 1
+        if seen[j] == 2:
+            ready.append(j)
+        if at + 1 == len(arrivals) or arrivals[at + 1][1].bit_count() > j.bit_count():
+            for k in ready:
+                project(k)
+            ready = []
+            if j.bit_count() == 1:
+                for k in range(2):
+                    chunk(1, k, 0)
+    for h in range(2):
+        for j in range(1, n):
+            for t in range(2):
+                sum_copy(t, h, j).wait_send()
+            hid_copy(h, j ^ (1 << tree.first(h, j)), j).wait_send()
+
+
+def middle(n, call, x_cols, d_cols, w_up, w_down, placed):
+    rows, wide = placed.shape
+    half = wide // 2
+    depth = w_down.shape[1]
+    vmem = pl.BlockSpec(memory_space=pltpu.VMEM)
+    return pl.pallas_call(
+        functools.partial(middle_kernel, n),
+        out_shape=(
+            jax.ShapeDtypeStruct((n * rows, depth), BF16),
+            jax.ShapeDtypeStruct((rows, wide), BF16),
+        ),
+        in_specs=[vmem] * 5,
+        out_specs=(vmem, vmem),
+        scratch_shapes=[
+            pltpu.VMEM((2, 2, n, rows, half), BF16),
+            pltpu.VMEM((2, 2, n, rows, half), BF16),
+            pltpu.VMEM((2, n, rows, half), BF16),
+            pltpu.VMEM((2, rows, half), F32),
+            pltpu.SemaphoreType.DMA((2, 2, n)),
+            pltpu.SemaphoreType.DMA((2, 2, n)),
+            pltpu.SemaphoreType.DMA((2, n)),
+            pltpu.SemaphoreType.DMA((2, n)),
+        ],
+        compiler_params=pltpu.CompilerParams(
+            collective_id=call, has_side_effects=True, vmem_limit_bytes=VMEM_LIMIT
+        ),
+        cost_estimate=pl.CostEstimate(
+            flops=6 * n * rows * wide * depth, bytes_accessed=4 * wide * depth, transcendentals=2 * rows * wide
+        ),
+        name="middle",
+    )(x_cols, d_cols, w_up, w_down, placed)
+
+
+def passes_of(n, rows, wide, depth):
+    count = 1
+    while True:
+        r = rows // count
+        need = 10 * n * r * wide * 2 // 2 + 4 * wide * depth + 4 * n * r * depth + 12 * r * wide + 2 * n * r * depth
+        if need <= VMEM_PLAN or r % 32:
+            return count
+        count *= 2
 
 
 def on_device(
@@ -34,28 +243,36 @@
     blocks = lax.all_gather(delta.astype(jnp.bfloat16), "shard", axis=0, tiled=True)
     x_cols = lax.all_to_all(gathered_x, "shard", split_axis=1, concat_axis=0, tiled=True)
     d_cols = lax.all_to_all(gathered_d, "shard", split_axis=1, concat_axis=0, tiled=True)
-    pre_part = jnp.dot(x_cols, w_up, preferred_element_type=jnp.float32).astype(jnp.bfloat16)
-    pre = lax.psum_scatter(pre_part, "shard", scatter_dimension=0, tiled=True).astype(jnp.float32)
-    back_part = lax.dot_general(
-        d_cols, w_down, (((1,), (1,)), ((), ())), preferred_element_type=jnp.float32
-    ).astype(jnp.bfloat16)
-    back = lax.psum_scatter(back_part, "shard", scatter_dimension=0, tiled=True).astype(jnp.float32)
     x_blocks = gathered_x.reshape(rows, row_count, side)
     picked = jnp.einsum(
         "rkb,sk->srb", x_blocks, row_onehot.astype(jnp.bfloat16), preferred_element_type=jnp.float32
     ).astype(jnp.bfloat16)
     contrib = jnp.einsum("srb,sbn->srn", picked, blocks, preferred_element_type=jnp.float32)
     placed = jnp.einsum("srn,sc->rcn", contrib, col_onehot, precision=lax.Precision.HIGHEST)
-    pre = pre + placed.reshape(rows, local_ff)
-    hidden = jax.nn.silu(pre).astype(jnp.bfloat16)
-    hidden_all = lax.all_gather(hidden, "shard", axis=0, tiled=True)
-    partial_out = jnp.dot(hidden_all, w_down, preferred_element_type=jnp.float32)
-    partial_out = partial_out.astype(jnp.bfloat16).reshape(shards, lax.axis_size("dp"), -1, w_down.shape[1])
+    placed = placed.reshape(rows, local_ff)
+    passes = passes_of(shards, rows, local_ff, w_down.shape[1])
+    piece = rows // passes
+    x_cols = x_cols.reshape(shards, passes, piece, -1)
+    d_cols = d_cols.reshape(shards, passes, piece, -1)
+    outs, slopes = [], []
+    for p in range(passes):
+        out, slope = middle(
+            shards,
+            p,
+            x_cols[:, p].reshape(shards * piece, -1),
+            d_cols[:, p].reshape(shards * piece, -1),
+            w_up,
+            w_down,
+            placed[p * piece : (p + 1) * piece],
+        )
+        outs.append(out.reshape(shards, piece, -1))
+        slopes.append(slope)
+    partial_out = jnp.concatenate(outs, axis=1)
+    dpre = jnp.concatenate(slopes, axis=0)
+    partial_out = partial_out.reshape(shards, lax.axis_size("dp"), -1, w_down.shape[1])
     partial_out = partial_out.transpose(1, 0, 2, 3).reshape(-1, w_down.shape[1])
     out_cols = lax.psum_scatter(partial_out, "dp", scatter_dimension=0, tiled=True)
     layer_out = lax.all_to_all(out_cols, "shard", split_axis=0, concat_axis=1, tiled=True)
-    sigma = jax.nn.sigmoid(pre)
-    dpre = (back * sigma * (1.0 + pre * (1.0 - sigma))).astype(jnp.bfloat16)
     factor = 1.0 / math.sqrt(rows * shards)
     slope_blocks = dpre.reshape(rows, col_count, side)
     chosen = jnp.einsum(

time: 377 us -> 301 us (0.80)
  waiting for transfers between devices: 266 us -> 130 us
  Pallas kernels: 0 us -> 114 us
  blocking collectives: 38.9 us -> 0 us
  matrix products: 31.8 us -> 9.79 us
  starting transfers between devices: 4.16 us -> 11.7 us
    reduce_scatter x2 -> x0, waiting for transfers between devices: 127 us -> none  [the longest x1 70.5 us: on_device(): lax.psum_scatter(back_part, 'shard', scatter_dimension=0, tiled=True)]
    pallas_call x0 -> x1, Pallas kernels: none -> 114 us  [middle(): pl.pallas_call(functools.partial(middle_kernel, n), out_shape=(jax.ShapeD...]
    all_gather x1 -> x0, waiting for transfers between devices: 49.9 us -> none  [on_device(): hidden_all = lax.all_gather(hidden, 'shard', axis=0, tiled=True)]
    all_to_all x2 -> x0, blocking collectives: 38.9 us -> none  [the longest x1 20.1 us: on_device(): lax.all_to_all(gathered_d, 'shard', split_axis=1, concat_axis=0, tiled=True)]
    dot_general x3 -> x0, matrix products: 24.3 us -> none  [the longest x1 8.19 us: on_device(): lax.dot_general(d_cols, w_down, (((1,), (1,)), ((), ())), preferred_eleme...]
    all_gather x1, waiting for transfers between devices: 0.02 us -> 22.6 us  [on_device(): lax.all_gather(cotangent, 'dp', axis=0, tiled=True)]
    all_gather x1, waiting for transfers between devices: 0.02 us -> 18.6 us  [on_device(): lax.all_gather(delta.astype(jnp.bfloat16), 'shard', axis=0, tiled=True)]
    all_to_all x0 -> x2, starting transfers between devices: none -> 7.9 us  [the longest x1 4.24 us: on_device(): lax.all_to_all(gathered_d, 'shard', split_axis=1, concat_axis=0, tiled=True)]
  transfers between devices with their start and end apart: 9 -> 8, of which waited for: 6 -> 5; matrix products, arithmetic and copies ran while one was open for 10% -> 9% of each run, Pallas kernels for 0% -> 0%
where the time goes in v2:
time: 301 us; the launch traced here: 300 us
  waiting for transfers between devices  130 us (43%)
  Pallas kernels  114 us (38%)
  local copies, waits for them, and re-layouts  17.5 us (6%)
  between operations  13.9 us (5%)
  starting transfers between devices  11.7 us (4%)
  matrix products  9.79 us (3%)
  other arithmetic  3.58 us (1%)
    pallas_call x1, Pallas kernels, middle(): pl.pallas_call(functools.partial(middle_kernel, n), out_shape=(jax.ShapeD...  114 us
    reduce_scatter x1, waiting for transfers between devices, on_device(): lax.psum_scatter(grads.astype(jnp.bfloat16), 'shard', scatter_dimension=0...  34.4 us
    all_gather x1, waiting for transfers between devices, on_device(): lax.all_gather(tokens, 'dp', axis=0, tiled=True)  29.9 us
    reduce_scatter x1, waiting for transfers between devices, on_device(): lax.psum_scatter(partial_out, 'dp', scatter_dimension=0, tiled=True)  23.2 us
    all_gather x1, waiting for transfers between devices, on_device(): lax.all_gather(cotangent, 'dp', axis=0, tiled=True)  22.6 us
    all_gather x1, waiting for transfers between devices, on_device(): lax.all_gather(delta.astype(jnp.bfloat16), 'shard', axis=0, tiled=True)  18.6 us
  transfers between devices with their start and end apart: 8, of which 5 were waited for; matrix products, arithmetic and copies ran while one was open for 9% of the time, Pallas kernels for 0%

profile of v2, /device:TPU:0, one launch (start us, length us, event | category | flops | bytes accessed | tf_op | source)
XLA Modules:
  0.0 300.3 jit_solution(16435663164781413580)
XLA Ops:
  7.2 0.0 all-gather.4.cloned.1.call-start
  7.2 0.7 all-gather.4.cloned.1.call-update
  7.9 0.0 all-gather.6.cloned.1.call-start
  7.9 0.7 all-gather.6.cloned.1.call-update
  8.6 0.0 all-gather.8.cloned.1.call-start
  8.7 1.6 convert_element_type.32
  10.3 0.0 all-gather.8.cloned.1.call-update
  10.3 29.9 %all-gather.4.cloned.1.call-done = bf16[128,4096]{1,0:T(8,128)(2,1)} async-done(((bf16[32,4096]{1,0:T(8,128)(2,1)}), bf16[128,4096]{1,0:T(8,128)(2,1)}) %all-gather.4.cloned.1.call-update) | async-done | bytes 1048592 | tf_op jit(solution)/shard_map/all_gather | solution.py:225
  40.2 2.4 copy.65
  42.6 3.7 %all-to-all-start = ((bf16[128,8,512]{2,0,1:T(8,128)(2,1)}), bf16[128,8,512]{2,0,1:T(8,128)(2,1)S(1)}, u32[]{:S(2)}, u32[]{:S(2)}) async-start(bf16[128,8,512]{2,0,1:T(8,128)(2,1)} %bitcast.41), calls=%async_computation | async-start | bytes 2097152 | tf_op jit(solution)/shard_map/all_to_all | solution.py:244
  46.3 0.0 copy-done.8
  46.3 0.1 dynamic_slice.11
  46.4 0.0 copy-done.6
  46.4 0.1 dynamic-slice_convert_fusion
  46.4 0.2 copy.55
  46.7 22.6 %all-gather.6.cloned.1.call-done = bf16[128,4096]{1,0:T(8,128)(2,1)} async-done(((bf16[32,4096]{1,0:T(8,128)(2,1)}), bf16[128,4096]{1,0:T(8,128)(2,1)}) %all-gather.6.cloned.1.call-update) | async-done | bytes 1048592 | tf_op jit(solution)/shard_map/all_gather | solution.py:226
  69.3 2.3 copy.64
  71.6 0.0 all-to-all-done
  71.6 4.2 %all-to-all-start.1 = ((bf16[128,8,512]{2,0,1:T(8,128)(2,1)}), bf16[128,8,512]{2,0,1:T(8,128)(2,1)}, u32[]{:S(2)}, u32[]{:S(2)}) async-start(bf16[128,8,512]{2,0,1:T(8,128)(2,1)} %bitcast.40), calls=%async_computation.1 | async-start | bytes 2097152 | tf_op jit(solution)/shard_map/all_to_all | solution.py:245
  75.8 0.0 reduce-scatter.3.cloned.1.call-start
  75.9 1.4 convolution_convert_fusion.1
  77.3 1.9 copy.48
  79.3 18.6 %all-gather.8.cloned.1.call-done = bf16[32,128,128]{2,1,0:T(8,128)(2,1)} async-done(((bf16[4,128,128]{2,1,0:T(8,128)(2,1)}), bf16[32,128,128]{2,1,0:T(8,128)(2,1)}) %all-gather.8.cloned.1.call-update) | async-done | bytes 1048592 | tf_op jit(solution)/shard_map/all_gather | solution.py:243
  97.9 1.7 fusion.23
  99.6 4.4 %fusion.2 = f32[128,28,128]{2,1,0:T(8,128)} fusion(f32[32,128,128]{2,1,0:T(8,128)S(1)} %fusion.23, f32[32]{0:T(128)S(1)} %get-tuple-element.11, s32[32]{0:T(128)S(1)} %get-tuple-element.12), kind=kOutput, calls=%fused_computation.3 | convolution fusion | flops 176162560 | bytes 3932416 | tf_op jit(solution)/shard_map/srn,sc->rcn/dot_general | solution.py:251
  104.0 2.9 copy.42
  106.9 2.8 copy.43.placed_ref
  109.7 0.0 all-to-all-done.1
  109.7 113.6 %middle.1 = (bf16[1024,512]{1,0:T(8,128)(2,1)}, bf16[128,3584]{1,0:T(8,128)(2,1)}) custom-call(bf16[1024,512]{1,0:T(8,128)(2,1)} %bitcast.48, bf16[1024,512]{1,0:T(8,128)(2,1)} %bitcast.3.d_ref, bf16[512,3584]{1,0:T(8,128)(2,1)} %up_ref.1, bf16[3584,512]{1,0:T(8,128)(2,1)} %down_ref.1, f32[128,3584]{1,0:T(8,128)} %copy.43.placed_ref), custom_call_target="tpu_custom_call" | custom-call | flops 11274289152 | bytes 7340032 | tf_op jit(solution)/shard_map/middle/pallas_call | solution.py:180
  223.3 2.4 copy.44
  225.7 0.0 reduce-scatter.3.cloned.1.call-update
  225.7 0.0 reduce-scatter.5.cloned.1.call-start
  225.8 0.6 copy.46
  226.4 1.1 copy.47
  227.5 0.5 convolution_convert_fusion
  228.0 0.0 copy-start.2
  228.0 0.0 copy-start.4
  228.0 0.0 copy-start.5
  228.1 1.8 multiply_convert_fusion
  229.8 0.0 reduce-scatter.5.cloned.1.call-update
  229.8 23.2 %reduce-scatter.3.cloned.1.call-done = bf16[256,512]{1,0:T(8,128)(2,1)} async-done(((bf16[1024,512]{1,0:T(8,128)(2,1)}), bf16[256,512]{1,0:T(8,128)(2,1)}) %reduce-scatter.3.cloned.1.call-update) | async-done | bytes 262160 | tf_op jit(solution)/shard_map/reduce_scatter | solution.py:274
  253.0 3.7 %all-to-all-start.2 = ((bf16[8,32,512]{2,1,0:T(8,128)(2,1)}), bf16[8,32,512]{2,1,0:T(8,128)(2,1)S(1)}, u32[]{:S(2)}, u32[]{:S(2)}) async-start(bf16[8,32,512]{2,1,0:T(8,128)(2,1)} %bitcast.52), calls=%async_computation.3 | async-start | bytes 524288 | tf_op jit(solution)/shard_map/all_to_all | solution.py:275
  256.7 34.4 %reduce-scatter.5.cloned.1.call-done = bf16[4,128,128]{2,1,0:T(8,128)(2,1)} async-done(((bf16[32,128,128]{2,1,0:T(8,128)(2,1)}), bf16[4,128,128]{2,1,0:T(8,128)(2,1)}) %reduce-scatter.5.cloned.1.call-update) | async-done | bytes 131088 | tf_op jit(solution)/shard_map/reduce_scatter | solution.py:286
  291.1 0.0 copy-done.2
  291.1 0.0 copy-done.5
  291.1 1.9 divide_subtract_fusion
  293.0 0.0 all-to-all-done.2
  293.0 0.7 copy.54
  (11 shorter events, 0.0 us)
Async XLA Ops:
  7.2 33.1 %all-gather.4.cloned.1.call-start = ((), (), s32[]{:S(2)}) async-start(), calls=%async_computation.5 | async-start | bytes 1310720 | tf_op jit(solution)/shard_map/all_gather | solution.py:225
  7.9 61.4 %all-gather.6.cloned.1.call-start = ((), (), s32[]{:S(2)}) async-start(), calls=%async_computation.6 | async-start | bytes 1310720 | tf_op jit(solution)/shard_map/all_gather | solution.py:226
  8.6 89.2 %all-gather.8.cloned.1.call-start = ((), (), s32[]{:S(2)}) async-start(), calls=%async_computation.7 | async-start | bytes 1179648 | tf_op jit(solution)/shard_map/all_gather | solution.py:243
  40.2 6.0 %copy-start.8 = (s32[128]{0:T(128)S(1)}, s32[128]{0:T(128)}, u32[]{:S(2)}) copy-start(s32[128]{0:T(128)} %param.17) | copy-start | bytes 1540
  40.2 6.1 %copy-start.6 = (s32[128]{0:T(128)S(1)}, s32[128]{0:T(128)}, u32[]{:S(2)}) copy-start(s32[128]{0:T(128)} %param.19) | copy-start | bytes 1540
  40.2 6.1 %copy-start.7 = (s32[128]{0:T(128)S(1)}, s32[128]{0:T(128)}, u32[]{:S(2)}) copy-start(s32[128]{0:T(128)} %param.18) | copy-start | bytes 1540
  40.2 6.2 %copy-start = (bf16[128,4096]{1,0:T(8,128)(2,1)S(1)}, bf16[128,4096]{1,0:T(8,128)(2,1)}, u32[]{:S(2)}) copy-start(bf16[128,4096]{1,0:T(8,128)(2,1)} %all-gather.4.cloned.1.call-done) | copy-start | bytes 3145732
  42.6 29.0 %all-to-all-start = ((bf16[128,8,512]{2,0,1:T(8,128)(2,1)}), bf16[128,8,512]{2,0,1:T(8,128)(2,1)S(1)}, u32[]{:S(2)}, u32[]{:S(2)}) async-start(bf16[128,8,512]{2,0,1:T(8,128)(2,1)} %bitcast.41), calls=%async_computation | async-start | bytes 2097152 | tf_op jit(solution)/shard_map/all_to_all | solution.py:244
  71.6 4.3 %copy-start.1 = (bf16[128,8,512]{2,0,1:T(8,128)(2,1)}, bf16[128,8,512]{2,0,1:T(8,128)(2,1)S(1)}, u32[]{:S(2)}) copy-start(bf16[128,8,512]{2,0,1:T(8,128)(2,1)S(1)} %all-to-all-done) | copy-start | bytes 3145732
  71.6 38.1 %all-to-all-start.1 = ((bf16[128,8,512]{2,0,1:T(8,128)(2,1)}), bf16[128,8,512]{2,0,1:T(8,128)(2,1)}, u32[]{:S(2)}, u32[]{:S(2)}) async-start(bf16[128,8,512]{2,0,1:T(8,128)(2,1)} %bitcast.40), calls=%async_computation.1 | async-start | bytes 2097152 | tf_op jit(solution)/shard_map/all_to_all | solution.py:245
  75.8 177.2 %reduce-scatter.3.cloned.1.call-start = ((), (), s32[]{:S(2)}) async-start(), calls=%async_computation.8 | async-start | bytes 1310720 | tf_op jit(solution)/shard_map/reduce_scatter | solution.py:274
  223.3 2.5 copy-start.3
  225.7 65.4 %reduce-scatter.5.cloned.1.call-start = ((), (), s32[]{:S(2)}) async-start(), calls=%async_computation.9 | async-start | bytes 1179648 | tf_op jit(solution)/shard_map/reduce_scatter | solution.py:286
  228.0 63.1 %copy-start.2 = (f32[4,128,128]{2,1,0:T(8,128)S(1)}, f32[4,128,128]{2,1,0:T(8,128)}, u32[]{:S(2)}) copy-start(f32[4,128,128]{2,1,0:T(8,128)} %param.14) | copy-start | bytes 786436
  228.0 63.1 %copy-start.4 = (f32[4,128,128]{2,1,0:T(8,128)S(1)}, f32[4,128,128]{2,1,0:T(8,128)}, u32[]{:S(2)}) copy-start(f32[4,128,128]{2,1,0:T(8,128)} %param.15) | copy-start | bytes 786436
  228.0 63.1 %copy-start.5 = (f32[4,128,128]{2,1,0:T(8,128)S(1)}, f32[4,128,128]{2,1,0:T(8,128)}, u32[]{:S(2)}) copy-start(f32[4,128,128]{2,1,0:T(8,128)} %param.16) | copy-start | bytes 786436
  253.0 40.0 %all-to-all-start.2 = ((bf16[8,32,512]{2,1,0:T(8,128)(2,1)}), bf16[8,32,512]{2,1,0:T(8,128)(2,1)S(1)}, u32[]{:S(2)}, u32[]{:S(2)}) async-start(bf16[8,32,512]{2,1,0:T(8,128)(2,1)} %bitcast.52), calls=%async_computation.3 | async-start | bytes 524288 | tf_op jit(solution)/shard_map/all_to_all | solution.py:275
Sparse Core Ops, SparseCore 0:
  9.6 30.6 all-gather.3
  41.8 27.4 all-gather.5
  71.7 26.1 all-gather.7
  225.8 27.1 reduce-scatter.2
  256.4 34.7 reduce-scatter.4

commit v3 on v2

--- a/solution.py
+++ b/solution.py
@@ -49,9 +49,200 @@
     return tile
 
 
+def meet(n, groups, me, group):
+    barrier = pltpu.get_barrier_semaphore()
+    for j in range(1, n):
+        pl.semaphore_signal(
+            barrier, inc=1, device_id={"shard": flip(me, j)}, device_id_type=pl.DeviceIdType.MESH
+        )
+    for k in range(1, groups):
+        pl.semaphore_signal(
+            barrier, inc=1, device_id={"dp": (group + k) % groups}, device_id_type=pl.DeviceIdType.MESH
+        )
+    pl.semaphore_wait(barrier, n - 1 + groups - 1)
+
+
+def group_copies(source, target, groups, group, send_s, recv_s):
+    return [
+        pltpu.make_async_remote_copy(
+            src_ref=source,
+            dst_ref=target(),
+            send_sem=send_s.at[k],
+            recv_sem=recv_s.at[k],
+            device_id={"dp": (group + k) % groups},
+            device_id_type=pl.DeviceIdType.MESH,
+        )
+        for k in range(1, groups)
+    ]
+
+
+def front_kernel(
+    n, tok_ref, blk_ref, rows_ref, cols_ref, all_ref, zsend_s, zrecv_s, send_s, recv_s, bsend_s, brecv_s
+):
+    me = lax.axis_index("shard")
+    group = lax.axis_index("dp")
+    groups = rows_ref.shape[0]
+    depth = cols_ref.shape[3]
+    meet(n, groups, me, group)
+    z_copies = group_copies(tok_ref, lambda: rows_ref.at[group], groups, group, zsend_s, zrecv_s)
+    for copy in z_copies:
+        copy.start()
+
+    def blk_copy(j):
+        return pltpu.make_async_remote_copy(
+            src_ref=blk_ref,
+            dst_ref=all_ref.at[me],
+            send_sem=bsend_s.at[j],
+            recv_sem=brecv_s.at[j],
+            device_id={"shard": flip(me, j)},
+            device_id_type=pl.DeviceIdType.MESH,
+        )
+
+    def col_copy(j):
+        there = flip(me, j)
+        return pltpu.make_async_remote_copy(
+            src_ref=rows_ref.at[:, :, pl.ds(pl.multiple_of(there * depth, 128), depth)],
+            dst_ref=cols_ref.at[me],
+            send_sem=send_s.at[j],
+            recv_sem=recv_s.at[j],
+            device_id={"shard": there},
+            device_id_type=pl.DeviceIdType.MESH,
+        )
+
+    for j in range(1, n):
+        blk_copy(j).start()
+    rows_ref[group] = tok_ref[...]
+    all_ref[me] = blk_ref[...]
+    for copy in z_copies:
+        copy.wait_recv()
+    for j in range(n - 1, 0, -1):
+        col_copy(j).start()
+    cols_ref[me] = rows_ref[:, :, pl.ds(pl.multiple_of(me * depth, 128), depth)]
+    for j in range(1, n):
+        blk_copy(j).wait()
+        col_copy(j).wait()
+    for copy in z_copies:
+        copy.wait_send()
+
+
+def front(n, groups, call, tokens, blocks):
+    vmem = pl.BlockSpec(memory_space=pltpu.VMEM)
+    rows, width = tokens.shape
+    return pl.pallas_call(
+        functools.partial(front_kernel, n),
+        out_shape=(
+            jax.ShapeDtypeStruct((groups, rows, width), BF16),
+            jax.ShapeDtypeStruct((n, groups, rows, width // n), BF16),
+            jax.ShapeDtypeStruct((n,) + blocks.shape, BF16),
+        ),
+        in_specs=[vmem] * 2,
+        out_specs=(vmem,) * 3,
+        scratch_shapes=[pltpu.SemaphoreType.DMA((groups,))] * 2 + [pltpu.SemaphoreType.DMA((n,))] * 4,
+        compiler_params=pltpu.CompilerParams(
+            collective_id=call, has_side_effects=True, vmem_limit_bytes=VMEM_LIMIT // 2
+        ),
+        name="front",
+    )(tokens, blocks)
+
+
+def back_kernel(
+    n, part_ref, grad_ref, out_ref, sum_ref, zgot, ggot, mine, fin,
+    zsend_s, zrecv_s, gsend_s, grecv_s, send_s, recv_s,
+):
+    me = lax.axis_index("shard")
+    group = lax.axis_index("dp")
+    groups = part_ref.shape[0]
+    depth = part_ref.shape[3]
+    meet(n, groups, me, group)
+
+    def z_copy(k):
+        there = (group + k) % groups
+        return pltpu.make_async_remote_copy(
+            src_ref=part_ref.at[there],
+            dst_ref=zgot.at[k],
+            send_sem=zsend_s.at[k],
+            recv_sem=zrecv_s.at[k],
+            device_id={"dp": there},
+            device_id_type=pl.DeviceIdType.MESH,
+        )
+
+    def grad_copy(j):
+        there = flip(me, j)
+        return pltpu.make_async_remote_copy(
+            src_ref=grad_ref.at[there],
+            dst_ref=ggot.at[j],
+            send_sem=gsend_s.at[j],
+            recv_sem=grecv_s.at[j],
+            device_id={"shard": there},
+            device_id_type=pl.DeviceIdType.MESH,
+        )
+
+    def out_copy(j):
+        return pltpu.make_async_remote_copy(
+            src_ref=mine.at[flip(me, j)],
+            dst_ref=fin.at[me],
+            send_sem=send_s.at[j],
+            recv_sem=recv_s.at[j],
+            device_id={"shard": flip(me, j)},
+            device_id_type=pl.DeviceIdType.MESH,
+        )
+
+    for k in range(1, groups):
+        z_copy(k).start()
+    for j in range(n - 1, 0, -1):
+        grad_copy(j).start()
+    total = grad_ref[me].astype(F32)
+    for j in range(1, n):
+        grad_copy(j).wait_recv()
+        total += ggot[j].astype(F32)
+    sum_ref[...] = total
+    total = part_ref[group].astype(F32)
+    for k in range(1, groups):
+        z_copy(k).wait_recv()
+        total += zgot[k].astype(F32)
+    mine[...] = total.astype(BF16)
+    for j in range(n - 1, 0, -1):
+        out_copy(j).start()
+    fin[me] = mine[me]
+    for j in range(1, n):
+        out_copy(j).wait()
+        grad_copy(j).wait_send()
+    for k in range(1, groups):
+        z_copy(k).wait_send()
+    for s in range(n):
+        out_ref[:, pl.ds(s * depth, depth)] = fin[s]
+
+
+def back(n, groups, call, part, grads):
+    vmem = pl.BlockSpec(memory_space=pltpu.VMEM)
+    _, _, rows, depth = part.shape
+    return pl.pallas_call(
+        functools.partial(back_kernel, n),
+        out_shape=(
+            jax.ShapeDtypeStruct((rows, n * depth), BF16),
+            jax.ShapeDtypeStruct(grads.shape[1:], F32),
+        ),
+        in_specs=[vmem] * 2,
+        out_specs=(vmem,) * 2,
+        scratch_shapes=[
+            pltpu.VMEM((groups, n, rows, depth), BF16),
+            pltpu.VMEM(grads.shape, BF16),
+            pltpu.VMEM((n, rows, depth), BF16),
+            pltpu.VMEM((n, rows, depth), BF16),
+        ]
+        + [pltpu.SemaphoreType.DMA((groups,))] * 2
+        + [pltpu.SemaphoreType.DMA((n,))] * 4,
+        compiler_params=pltpu.CompilerParams(
+            collective_id=call, has_side_effects=True, vmem_limit_bytes=VMEM_LIMIT // 2
+        ),
+        name="back",
+    )(part, grads)
+
+
 def middle_kernel(
-    n, x_ref, d_ref, up_ref, down_ref, placed_ref, out_ref, dpre_ref,
-    part, got, hid, pre_s, send_s, recv_s, hsend_s, hrecv_s,
+    n, x_ref, cot_ref, up_ref, down_ref, placed_ref, out_ref, dpre_ref,
+    part, got, hid, pre_s, cot_all, cot_cols,
+    send_s, recv_s, hsend_s, hrecv_s, zsend_s, zrecv_s, csend_s, crecv_s,
 ):
     tree = Tree(n)
     me = lax.axis_index("shard")
@@ -60,12 +251,10 @@
     tile = tile_of(half)
     tiles = half // tile
 
-    barrier = pltpu.get_barrier_semaphore()
-    for b in range(tree.bits):
-        pl.semaphore_signal(
-            barrier, inc=1, device_id={"shard": flip(me, 1 << b)}, device_id_type=pl.DeviceIdType.MESH
-        )
-    pl.semaphore_wait(barrier, tree.bits)
+    groups = cot_all.shape[0]
+    depth = down_ref.shape[1]
+    group = lax.axis_index("dp")
+    meet(n, groups, me, group)
 
     def sum_copy(t, h, j):
         return pltpu.make_async_remote_copy(
@@ -77,6 +266,17 @@
             device_id_type=pl.DeviceIdType.MESH,
         )
 
+    def cot_copy(j):
+        there = flip(me, j)
+        return pltpu.make_async_remote_copy(
+            src_ref=cot_all.at[:, :, pl.ds(pl.multiple_of(there * depth, 128), depth)],
+            dst_ref=cot_cols.at[j],
+            send_sem=csend_s.at[j],
+            recv_sem=crecv_s.at[j],
+            device_id={"shard": there},
+            device_id_type=pl.DeviceIdType.MESH,
+        )
+
     def hid_copy(h, src, dst):
         return pltpu.make_async_remote_copy(
             src_ref=hid.at[h, src],
@@ -87,21 +287,28 @@
             device_id_type=pl.DeviceIdType.MESH,
         )
 
+    landed = set()
+
     def chunk(t, h, j):
-        source = x_ref if t == 0 else d_ref
         at = pl.ds(pl.multiple_of(flip(me, j) * rows, rows), rows)
         kids = tree.children(h, j)
         for kid in kids:
             sum_copy(t, h, kid).wait_recv()
+        if t == 1 and j and j not in landed:
+            landed.add(j)
+            cot_copy(j).wait_recv()
 
         def body(i, _):
             cols = pl.ds(pl.multiple_of(i * tile, 128), tile)
             wide = pl.ds(pl.multiple_of(h * half + i * tile, 128), tile)
             if t == 0:
-                total = jnp.dot(source[at, :], up_ref[:, wide], preferred_element_type=F32)
+                total = jnp.dot(x_ref[at, :], up_ref[:, wide], preferred_element_type=F32)
             else:
                 total = lax.dot_general(
-                    source[at, :], down_ref[wide, :], (((1,), (1,)), ((), ())), preferred_element_type=F32
+                    cot_cols[j].reshape(rows, depth),
+                    down_ref[wide, :],
+                    (((1,), (1,)), ((), ())),
+                    preferred_element_type=F32,
                 )
             for kid in kids:
                 total = total + got[t, h, kid, :, cols].astype(F32)
@@ -132,39 +339,50 @@
     even.sort(key=lambda c: (-c[1].bit_count(), len(tree.children(*c))))
     early = [c for c in even if len(tree.children(*c)) == 1]
     late = [c for c in even if len(tree.children(*c)) > 1]
-    for t in range(2):
-        for j in odd:
-            for h in range(2):
-                chunk(t, h, j)
+    cot_all[group] = cot_ref[...]
+    z_copies = group_copies(cot_ref, lambda: cot_all.at[group], groups, group, zsend_s, zrecv_s)
+    for copy in z_copies:
+        copy.start()
+    for j in odd:
+        for h in range(2):
+            chunk(0, h, j)
     for h, j in even:
         chunk(0, h, j)
-    for h, j in early:
-        chunk(1, h, j)
+    for copy in z_copies:
+        copy.wait_recv()
+    for j in odd + sorted({j for _, j in even}, key=lambda j: -j.bit_count()):
+        cot_copy(j).start()
+    cot_cols[0] = cot_all[:, :, pl.ds(pl.multiple_of(me * depth, 128), depth)]
     for h in range(2):
         chunk(0, h, 0)
         for j in sorted(tree.children(h, 0), key=lambda j: -len(tree.children(h, j))):
             hid_copy(h, 0, j).start()
-    for h, j in late:
+    for j in odd:
+        for h in range(2):
+            chunk(1, h, j)
+    for h, j in early:
         chunk(1, h, j)
     project(0)
     arrivals = [(h, j) for j in range(1, n) for h in range(2)]
     arrivals.sort(key=lambda c: (c[1].bit_count(), -len(tree.children(*c))))
-    seen = [0] * n
-    ready = []
-    for at, (h, j) in enumerate(arrivals):
-        hid_copy(h, j ^ (1 << tree.first(h, j)), j).wait_recv()
-        for kid in sorted(tree.children(h, j), key=lambda k: -len(tree.children(h, k))):
-            hid_copy(h, j, kid).start()
-        seen[j] += 1
-        if seen[j] == 2:
-            ready.append(j)
-        if at + 1 == len(arrivals) or arrivals[at + 1][1].bit_count() > j.bit_count():
-            for k in ready:
-                project(k)
-            ready = []
-            if j.bit_count() == 1:
-                for k in range(2):
-                    chunk(1, k, 0)
+    for level in range(1, tree.bits + 1):
+        now = [c for c in arrivals if c[1].bit_count() == level]
+        for h, j in now:
+            hid_copy(h, j ^ (1 << tree.first(h, j)), j).wait_recv()
+            for kid in sorted(tree.children(h, j), key=lambda k: -len(tree.children(h, k))):
+                hid_copy(h, j, kid).start()
+        if level == 1:
+            for h, j in late:
+                chunk(1, h, j)
+        if level == min(2, tree.bits):
+            for h in range(2):
+                chunk(1, h, 0)
+        for j in sorted({j for _, j in now}):
+            project(j)
+    for copy in z_copies:
+        copy.wait_send()
+    for j in range(1, n):
+        cot_copy(j).wait_send()
     for h in range(2):
         for j in range(1, n):
             for t in range(2):
@@ -172,7 +390,7 @@
             hid_copy(h, j ^ (1 << tree.first(h, j)), j).wait_send()
 
 
-def middle(n, call, x_cols, d_cols, w_up, w_down, placed):
+def middle(n, groups, call, x_cols, cotangent, w_up, w_down, placed):
     rows, wide = placed.shape
     half = wide // 2
     depth = w_down.shape[1]
@@ -190,10 +408,16 @@
             pltpu.VMEM((2, 2, n, rows, half), BF16),
             pltpu.VMEM((2, n, rows, half), BF16),
             pltpu.VMEM((2, rows, half), F32),
+            pltpu.VMEM((groups,) + cotangent.shape, BF16),
+            pltpu.VMEM((n, groups, cotangent.shape[0], depth), BF16),
             pltpu.SemaphoreType.DMA((2, 2, n)),
             pltpu.SemaphoreType.DMA((2, 2, n)),
             pltpu.SemaphoreType.DMA((2, n)),
             pltpu.SemaphoreType.DMA((2, n)),
+            pltpu.SemaphoreType.DMA((groups,)),
+            pltpu.SemaphoreType.DMA((groups,)),
+            pltpu.SemaphoreType.DMA((n,)),
+            pltpu.SemaphoreType.DMA((n,)),
         ],
         compiler_params=pltpu.CompilerParams(
             collective_id=call, has_side_effects=True, vmem_limit_bytes=VMEM_LIMIT
@@ -202,14 +426,14 @@
             flops=6 * n * rows * wide * depth, bytes_accessed=4 * wide * depth, transcendentals=2 * rows * wide
         ),
         name="middle",
-    )(x_cols, d_cols, w_up, w_down, placed)
+    )(x_cols, cotangent, w_up, w_down, placed)
 
 
 def passes_of(n, rows, wide, depth):
     count = 1
     while True:
         r = rows // count
-        need = 10 * n * r * wide * 2 // 2 + 4 * wide * depth + 4 * n * r * depth + 12 * r * wide + 2 * n * r * depth
+        need = 10 * n * r * wide * 2 // 2 + 4 * wide * depth + 8 * n * r * depth + 12 * r * wide + 2 * n * r * depth
         if need <= VMEM_PLAN or r % 32:
             return count
         count *= 2
@@ -221,10 +445,10 @@
     shards = lax.axis_size("shard")
     own_slots = delta.shape[0]
     side = delta.shape[1]
-    gathered_x, gathered_d = (
-        lax.all_gather(tokens, "dp", axis=0, tiled=True),
-        lax.all_gather(cotangent, "dp", axis=0, tiled=True),
-    )
+    groups = lax.axis_size("dp")
+    gathered_x, x_cols, blocks = front(shards, groups, 0, tokens, delta.astype(BF16))
+    gathered_x = gathered_x.reshape(-1, tokens.shape[1])
+    blocks = blocks.reshape(-1, side, side)
     rows = gathered_x.shape[0]
     width = gathered_x.shape[1]
     local_ff = w_up.shape[1]
@@ -240,9 +464,6 @@
     col_onehot = (slot_col[:, None] == jnp.arange(col_count)[None, :]).astype(
         jnp.float32
     ) * slot_live[:, None]
-    blocks = lax.all_gather(delta.astype(jnp.bfloat16), "shard", axis=0, tiled=True)
-    x_cols = lax.all_to_all(gathered_x, "shard", split_axis=1, concat_axis=0, tiled=True)
-    d_cols = lax.all_to_all(gathered_d, "shard", split_axis=1, concat_axis=0, tiled=True)
     x_blocks = gathered_x.reshape(rows, row_count, side)
     picked = jnp.einsum(
         "rkb,sk->srb", x_blocks, row_onehot.astype(jnp.bfloat16), preferred_element_type=jnp.float32
@@ -251,28 +472,26 @@
     placed = jnp.einsum("srn,sc->rcn", contrib, col_onehot, precision=lax.Precision.HIGHEST)
     placed = placed.reshape(rows, local_ff)
     passes = passes_of(shards, rows, local_ff, w_down.shape[1])
-    piece = rows // passes
-    x_cols = x_cols.reshape(shards, passes, piece, -1)
-    d_cols = d_cols.reshape(shards, passes, piece, -1)
+    piece = tokens.shape[0] // passes
+    depth = w_down.shape[1]
+    x_cols = x_cols.reshape(shards, groups, passes, piece, depth)
+    placed = placed.reshape(groups, passes, piece, local_ff)
     outs, slopes = [], []
     for p in range(passes):
         out, slope = middle(
             shards,
-            p,
-            x_cols[:, p].reshape(shards * piece, -1),
-            d_cols[:, p].reshape(shards * piece, -1),
+            groups,
+            2 + p,
+            x_cols[:, :, p].reshape(-1, depth),
+            cotangent[p * piece : (p + 1) * piece],
             w_up,
             w_down,
-            placed[p * piece : (p + 1) * piece],
-        )
-        outs.append(out.reshape(shards, piece, -1))
-        slopes.append(slope)
-    partial_out = jnp.concatenate(outs, axis=1)
-    dpre = jnp.concatenate(slopes, axis=0)
-    partial_out = partial_out.reshape(shards, lax.axis_size("dp"), -1, w_down.shape[1])
-    partial_out = partial_out.transpose(1, 0, 2, 3).reshape(-1, w_down.shape[1])
-    out_cols = lax.psum_scatter(partial_out, "dp", scatter_dimension=0, tiled=True)
-    layer_out = lax.all_to_all(out_cols, "shard", split_axis=0, concat_axis=1, tiled=True)
+            placed[:, p].reshape(-1, local_ff),
+        )
+        outs.append(out.reshape(shards, groups, piece, depth))
+        slopes.append(slope.reshape(groups, piece, local_ff))
+    partial_out = jnp.concatenate(outs, axis=2).transpose(1, 0, 2, 3)
+    dpre = jnp.concatenate(slopes, axis=1)
     factor = 1.0 / math.sqrt(rows * shards)
     slope_blocks = dpre.reshape(rows, col_count, side)
     chosen = jnp.einsum(
@@ -283,9 +502,8 @@
     ).astype(jnp.bfloat16)
     grads = jnp.einsum("srk,srn->skn", picked, chosen, preferred_element_type=jnp.float32)
     grads = grads * factor
-    owned_grad = lax.psum_scatter(
-        grads.astype(jnp.bfloat16), "shard", scatter_dimension=0, tiled=True
-    ).astype(jnp.float32)
+    grads = grads.astype(BF16).reshape((shards,) + delta.shape)
+    layer_out, owned_grad = back(shards, groups, 1, partial_out, grads)
     new_first = 0.9 * first_moment + 0.1 * owned_grad
     new_second = 0.95 * second_moment + 0.05 * owned_grad * owned_grad
     corrected_first = new_first / (1.0 - 0.9**10)

time: 301 us -> 219 us (0.73)
  waiting for transfers between devices: 130 us -> 0 us
  Pallas kernels: 114 us -> 188 us
  between operations: 13.9 us -> 0.79 us
  starting transfers between devices: 11.7 us -> 0 us
    all_gather x3 -> x0, waiting for transfers between devices: 71 us -> none  [the longest x1 29.9 us: on_device(): lax.all_gather(tokens, 'dp', axis=0, tiled=True)]
    pallas_call x0 -> x2, Pallas kernels: none -> 62.8 us  [the longest x1 37 us: front(): pl.pallas_call(functools.partial(front_kernel, n), out_shape=(jax.ShapeDt...]
    reduce_scatter x2 -> x0, waiting for transfers between devices: 57.6 us -> none  [the longest x1 34.4 us: on_device(): lax.psum_scatter(grads.astype(jnp.bfloat16), 'shard', scatter_dimension=0...]
    pallas_call x1, Pallas kernels: 114 us -> 126 us  [middle(): pl.pallas_call(functools.partial(middle_kernel, n), out_shape=(jax.ShapeD...]
    all_to_all x3 -> x0, starting transfers between devices: 11.6 us -> none  [the longest x1 4.24 us: on_device(): lax.all_to_all(gathered_d, 'shard', split_axis=1, concat_axis=0, tiled=True)]
    all_to_all x3 -> x0, local copies, waits for them, and re-layouts: 5.42 us -> none  [the longest x1 2.37 us: on_device(): lax.all_to_all(gathered_x, 'shard', split_axis=1, concat_axis=0, tiled=True)]
  transfers between devices with their start and end apart: 8 -> 0, of which waited for: 5 -> 0; matrix products, arithmetic and copies ran while one was open for 9% -> 0% of each run, Pallas kernels for 0% -> 0%
where the time goes in v3:
time: 219 us; the launch traced here: 216 us
  Pallas kernels  188 us (86%)
  local copies, waits for them, and re-layouts  15.6 us (7%)
  matrix products  8.8 us (4%)
  other arithmetic  2.69 us (1%)
    pallas_call x1, Pallas kernels, middle(): pl.pallas_call(functools.partial(middle_kernel, n), out_shape=(jax.ShapeD...  126 us
    pallas_call x1, Pallas kernels, front(): pl.pallas_call(functools.partial(front_kernel, n), out_shape=(jax.ShapeDt...  37 us
    pallas_call x1, Pallas kernels, back(): pl.pallas_call(functools.partial(back_kernel, n), out_shape=(jax.ShapeDty...  25.7 us

profile of v3, /device:TPU:0, one launch (start us, length us, event | category | flops | bytes accessed | tf_op | source)
XLA Modules:
  0.0 216.2 jit_solution(5358842771686433215)
XLA Ops:
  0.6 0.7 dynamic_slice.11
  1.4 0.7 dynamic-slice_convert_fusion
  2.1 1.0 convert_element_type.25.blk_ref
  3.1 0.0 copy-start
  3.1 0.9 copy-done
  4.0 37.0 %front.1 = (bf16[4,32,4096]{2,1,0:T(8,128)(2,1)S(1)}, bf16[8,4,32,512]{3,2,1,0:T(8,128)(2,1)S(1)}, bf16[8,4,128,128]{3,2,1,0:T(8,128)(2,1)S(1)}) custom-call(bf16[32,4096]{1,0:T(8,128)(2,1)S(1)} %copy-done, bf16[4,128,128]{2,1,0:T(8,128)(2,1)S(1)} %convert_element_type.25.blk_ref), custom_call_target="tpu_custom_call" | custom-call | tf_op jit(solution)/shard_map/front/pallas_call | solution.py:131
  41.1 0.0 copy-start.1
  41.1 0.2 copy.24
  41.3 0.7 copy-done.1
  42.1 1.4 convolution_convert_fusion
  43.5 1.9 copy.19
  45.4 0.5 fusion.21
  46.0 4.3 %fusion.2 = f32[128,28,128]{2,1,0:T(8,128)} fusion(f32[32,128,128]{2,1,0:T(8,128)S(1)} %fusion.21, f32[32]{0:T(128)S(1)} %get-tuple-element.21, s32[32]{0:T(128)S(1)} %get-tuple-element.22), kind=kOutput, calls=%fused_computation.4 | convolution fusion | flops 176162560 | bytes 3932416 | tf_op jit(solution)/shard_map/srn,sc->rcn/dot_general | solution.py:472
  50.3 2.9 %copy.15 = f32[128,28,128]{0,2,1:T(8,128)} copy(f32[128,28,128]{2,1,0:T(8,128)} %fusion.2) | data formatting | bytes 3670016 | tf_op jit(solution)/shard_map/srn,sc->rcn/transpose | solution.py:472
  53.2 2.8 %copy.16.placed_ref = f32[128,3584]{1,0:T(8,128)} copy(f32[128,3584]{0,1:T(8,128)} %bitcast.33) | data formatting | bytes 3670016 | tf_op jit(solution)/shard_map/reshape;squeeze;reshape;reshape | solution.py:489
  55.9 125.5 %middle.1 = (bf16[1024,512]{1,0:T(8,128)(2,1)}, bf16[128,3584]{1,0:T(8,128)(2,1)}) custom-call(bf16[1024,512]{1,0:T(8,128)(2,1)} %bitcast.32, bf16[32,4096]{1,0:T(8,128)(2,1)} %cot_ref.1, bf16[512,3584]{1,0:T(8,128)(2,1)} %up_ref.1, bf16[3584,512]{1,0:T(8,128)(2,1)} %down_ref.1, f32[128,3584]{1,0:T(8,128)} %copy.16.placed_ref), custom_call_target="tpu_custom_call" | custom-call | flops 11274289152 | bytes 7340032 | tf_op jit(solution)/shard_map/middle/pallas_call | solution.py:398
  181.5 1.3 copy.32
  182.8 1.6 copy.18
  184.4 1.9 copy.22
  186.2 1.7 fusion.9
  187.9 0.0 copy-start.2
  187.9 0.0 copy-start.3
  187.9 0.0 copy-start.4
  187.9 0.8 multiply_convert_fusion
  188.8 25.7 %back.1 = (bf16[32,4096]{1,0:T(8,128)(2,1)S(1)}, f32[4,128,128]{2,1,0:T(8,128)S(1)}) custom-call(bf16[4,8,32,512]{3,2,1,0:T(8,128)(2,1)S(1)} %bitcast.29, bf16[8,4,128,128]{3,2,1,0:T(8,128)(2,1)S(1)} %bitcast.28), custom_call_target="tpu_custom_call" | custom-call | tf_op jit(solution)/shard_map/back/pallas_call | solution.py:219
  214.5 0.0 copy-done.2
  214.5 0.0 copy-done.3
  214.5 0.0 copy-done.4
  214.5 1.0 divide_subtract_fusion
  215.5 0.7 copy.34
Async XLA Ops:
  3.1 1.0 copy-start
  41.1 1.0 copy-start.1
  187.9 26.6 %copy-start.2 = (f32[4,128,128]{2,1,0:T(8,128)S(1)}, f32[4,128,128]{2,1,0:T(8,128)}, u32[]{:S(2)}) copy-start(f32[4,128,128]{2,1,0:T(8,128)} %param.14) | copy-start | bytes 786436
  187.9 26.6 %copy-start.3 = (f32[4,128,128]{2,1,0:T(8,128)S(1)}, f32[4,128,128]{2,1,0:T(8,128)}, u32[]{:S(2)}) copy-start(f32[4,128,128]{2,1,0:T(8,128)} %param.15) | copy-start | bytes 786436
  187.9 26.6 %copy-start.4 = (f32[4,128,128]{2,1,0:T(8,128)S(1)}, f32[4,128,128]{2,1,0:T(8,128)}, u32[]{:S(2)}) copy-start(f32[4,128,128]{2,1,0:T(8,128)} %param.16) | copy-start | bytes 786436

commit v4 on v3

--- a/solution.py
+++ b/solution.py
@@ -98,13 +98,14 @@
             device_id_type=pl.DeviceIdType.MESH,
         )
 
-    def col_copy(j):
+    def col_copy(k, j):
         there = flip(me, j)
-        return pltpu.make_async_remote_copy(
-            src_ref=rows_ref.at[:, :, pl.ds(pl.multiple_of(there * depth, 128), depth)],
-            dst_ref=cols_ref.at[me],
-            send_sem=send_s.at[j],
-            recv_sem=recv_s.at[j],
+        source = (group + groups - k) % groups
+        return pltpu.make_async_remote_copy(
+            src_ref=rows_ref.at[source, :, pl.ds(pl.multiple_of(there * depth, 128), depth)],
+            dst_ref=cols_ref.at[me, source],
+            send_sem=send_s.at[k, j],
+            recv_sem=recv_s.at[k, j],
             device_id={"shard": there},
             device_id_type=pl.DeviceIdType.MESH,
         )
@@ -113,14 +114,16 @@
         blk_copy(j).start()
     rows_ref[group] = tok_ref[...]
     all_ref[me] = blk_ref[...]
-    for copy in z_copies:
-        copy.wait_recv()
-    for j in range(n - 1, 0, -1):
-        col_copy(j).start()
+    for k in range(groups):
+        if k:
+            z_copies[k - 1].wait_recv()
+        for j in range(n - 1, 0, -1):
+            col_copy(k, j).start()
     cols_ref[me] = rows_ref[:, :, pl.ds(pl.multiple_of(me * depth, 128), depth)]
     for j in range(1, n):
         blk_copy(j).wait()
-        col_copy(j).wait()
+        for k in range(groups):
+            col_copy(k, j).wait()
     for copy in z_copies:
         copy.wait_send()
 
@@ -137,7 +140,9 @@
         ),
         in_specs=[vmem] * 2,
         out_specs=(vmem,) * 3,
-        scratch_shapes=[pltpu.SemaphoreType.DMA((groups,))] * 2 + [pltpu.SemaphoreType.DMA((n,))] * 4,
+        scratch_shapes=[pltpu.SemaphoreType.DMA((groups,))] * 2
+        + [pltpu.SemaphoreType.DMA((groups, n))] * 2
+        + [pltpu.SemaphoreType.DMA((n,))] * 2,
         compiler_params=pltpu.CompilerParams(
             collective_id=call, has_side_effects=True, vmem_limit_bytes=VMEM_LIMIT // 2
         ),
@@ -146,25 +151,12 @@
 
 
 def back_kernel(
-    n, part_ref, grad_ref, out_ref, sum_ref, zgot, ggot, mine, fin,
-    zsend_s, zrecv_s, gsend_s, grecv_s, send_s, recv_s,
+    n, groups, mine_ref, grad_ref, out_ref, sum_ref, ggot, fin, gsend_s, grecv_s, send_s, recv_s
 ):
     me = lax.axis_index("shard")
     group = lax.axis_index("dp")
-    groups = part_ref.shape[0]
-    depth = part_ref.shape[3]
+    depth = mine_ref.shape[2]
     meet(n, groups, me, group)
-
-    def z_copy(k):
-        there = (group + k) % groups
-        return pltpu.make_async_remote_copy(
-            src_ref=part_ref.at[there],
-            dst_ref=zgot.at[k],
-            send_sem=zsend_s.at[k],
-            recv_sem=zrecv_s.at[k],
-            device_id={"dp": there},
-            device_id_type=pl.DeviceIdType.MESH,
-        )
 
     def grad_copy(j):
         there = flip(me, j)
@@ -179,7 +171,7 @@
 
     def out_copy(j):
         return pltpu.make_async_remote_copy(
-            src_ref=mine.at[flip(me, j)],
+            src_ref=mine_ref.at[flip(me, j)],
             dst_ref=fin.at[me],
             send_sem=send_s.at[j],
             recv_sem=recv_s.at[j],
@@ -187,37 +179,28 @@
             device_id_type=pl.DeviceIdType.MESH,
         )
 
-    for k in range(1, groups):
-        z_copy(k).start()
     for j in range(n - 1, 0, -1):
         grad_copy(j).start()
+    for j in range(n - 1, 0, -1):
+        out_copy(j).start()
+    fin[me] = mine_ref[me]
     total = grad_ref[me].astype(F32)
     for j in range(1, n):
         grad_copy(j).wait_recv()
         total += ggot[j].astype(F32)
     sum_ref[...] = total
-    total = part_ref[group].astype(F32)
-    for k in range(1, groups):
-        z_copy(k).wait_recv()
-        total += zgot[k].astype(F32)
-    mine[...] = total.astype(BF16)
-    for j in range(n - 1, 0, -1):
-        out_copy(j).start()
-    fin[me] = mine[me]
     for j in range(1, n):
         out_copy(j).wait()
         grad_copy(j).wait_send()
-    for k in range(1, groups):
-        z_copy(k).wait_send()
     for s in range(n):
         out_ref[:, pl.ds(s * depth, depth)] = fin[s]
 
 
-def back(n, groups, call, part, grads):
+def back(n, groups, call, mine, grads):
     vmem = pl.BlockSpec(memory_space=pltpu.VMEM)
-    _, _, rows, depth = part.shape
+    _, rows, depth = mine.shape
     return pl.pallas_call(
-        functools.partial(back_kernel, n),
+        functools.partial(back_kernel, n, groups),
         out_shape=(
             jax.ShapeDtypeStruct((rows, n * depth), BF16),
             jax.ShapeDtypeStruct(grads.shape[1:], F32),
@@ -225,28 +208,25 @@
         in_specs=[vmem] * 2,
         out_specs=(vmem,) * 2,
         scratch_shapes=[
-            pltpu.VMEM((groups, n, rows, depth), BF16),
             pltpu.VMEM(grads.shape, BF16),
             pltpu.VMEM((n, rows, depth), BF16),
-            pltpu.VMEM((n, rows, depth), BF16),
         ]
-        + [pltpu.SemaphoreType.DMA((groups,))] * 2
         + [pltpu.SemaphoreType.DMA((n,))] * 4,
         compiler_params=pltpu.CompilerParams(
             collective_id=call, has_side_effects=True, vmem_limit_bytes=VMEM_LIMIT // 2
         ),
         name="back",
-    )(part, grads)
+    )(mine, grads)
 
 
 def middle_kernel(
     n, x_ref, cot_ref, up_ref, down_ref, placed_ref, out_ref, dpre_ref,
-    part, got, hid, pre_s, cot_all, cot_cols,
-    send_s, recv_s, hsend_s, hrecv_s, zsend_s, zrecv_s, csend_s, crecv_s,
+    part, got, hid, pre_s, cot_all, cot_cols, outs, outs_got,
+    send_s, recv_s, hsend_s, hrecv_s, zsend_s, zrecv_s, csend_s, crecv_s, osend_s, orecv_s,
 ):
     tree = Tree(n)
     me = lax.axis_index("shard")
-    rows = placed_ref.shape[0]
+    rows, lane = placed_ref.shape[1:]
     half = part.shape[4]
     tile = tile_of(half)
     tiles = half // tile
@@ -301,6 +281,7 @@
         def body(i, _):
             cols = pl.ds(pl.multiple_of(i * tile, 128), tile)
             wide = pl.ds(pl.multiple_of(h * half + i * tile, 128), tile)
+            begin = h * (half // lane) + i * (tile // lane)
             if t == 0:
                 total = jnp.dot(x_ref[at, :], up_ref[:, wide], preferred_element_type=F32)
             else:
@@ -315,24 +296,38 @@
             if j:
                 part[t, h, j, :, cols] = total.astype(BF16)
             elif t == 0:
-                pre = total + placed_ref[:, wide]
+                pre = total + jnp.concatenate([placed_ref[begin + q] for q in range(tile // lane)], axis=1)
                 pre_s[h, :, cols] = pre
                 hid[h, 0, :, cols] = (pre * jax.nn.sigmoid(pre)).astype(BF16)
             else:
                 pre = pre_s[h, :, cols]
                 sigma = jax.nn.sigmoid(pre)
-                dpre_ref[:, wide] = (total * sigma * (1.0 + pre * (1.0 - sigma))).astype(BF16)
+                slope = (total * sigma * (1.0 + pre * (1.0 - sigma))).astype(BF16)
+                for q in range(tile // lane):
+                    dpre_ref[begin + q] = slope[:, q * lane : (q + 1) * lane]
             return 0
 
         lax.fori_loop(0, tiles, body, 0)
         if j:
             sum_copy(t, h, j).start()
 
+    def out_copy(j, k):
+        there = (group + k) % groups
+        return pltpu.make_async_remote_copy(
+            src_ref=outs.at[j, there],
+            dst_ref=outs_got.at[j, k],
+            send_sem=osend_s.at[j, k],
+            recv_sem=orecv_s.at[j, k],
+            device_id={"dp": there},
+            device_id_type=pl.DeviceIdType.MESH,
+        )
+
     def project(j):
-        at = pl.ds(pl.multiple_of(flip(me, j) * rows, rows), rows)
         total = jnp.dot(hid[0, j], down_ref[pl.ds(0, half), :], preferred_element_type=F32)
         total += jnp.dot(hid[1, j], down_ref[pl.ds(half, half), :], preferred_element_type=F32)
-        out_ref[at, :] = total.astype(BF16)
+        outs[j] = total.astype(BF16).reshape(outs.shape[1:])
+        for k in range(1, groups):
+            out_copy(j, k).start()
 
     odd = sorted((j for j in range(n) if j & 1), key=lambda j: -j.bit_count())
     even = [(h, j) for j in range(2, n, 2) for h in range(2)]
@@ -379,6 +374,15 @@
                 chunk(1, h, 0)
         for j in sorted({j for _, j in now}):
             project(j)
+    for j in sorted(range(n), key=lambda j: j.bit_count()):
+        total = outs[j, group].astype(F32)
+        for k in range(1, groups):
+            out_copy(j, k).wait_recv()
+            total += outs_got[j, k].astype(F32)
+        out_ref[flip(me, j)] = total.astype(BF16)
+    for j in range(n):
+        for k in range(1, groups):
+            out_copy(j, k).wait_send()
     for copy in z_copies:
         copy.wait_send()
     for j in range(1, n):
@@ -391,15 +395,17 @@
 
 
 def middle(n, groups, call, x_cols, cotangent, w_up, w_down, placed):
-    rows, wide = placed.shape
+    chunks, rows, lane = placed.shape
+    wide = chunks * lane
     half = wide // 2
+    piece = cotangent.shape[0]
     depth = w_down.shape[1]
     vmem = pl.BlockSpec(memory_space=pltpu.VMEM)
     return pl.pallas_call(
         functools.partial(middle_kernel, n),
         out_shape=(
-            jax.ShapeDtypeStruct((n * rows, depth), BF16),
-            jax.ShapeDtypeStruct((rows, wide), BF16),
+            jax.ShapeDtypeStruct((n, piece, depth), BF16),
+            jax.ShapeDtypeStruct(placed.shape, BF16),
         ),
         in_specs=[vmem] * 5,
         out_specs=(vmem, vmem),
@@ -409,7 +415,9 @@
             pltpu.VMEM((2, n, rows, half), BF16),
             pltpu.VMEM((2, rows, half), F32),
             pltpu.VMEM((groups,) + cotangent.shape, BF16),
-            pltpu.VMEM((n, groups, cotangent.shape[0], depth), BF16),
+            pltpu.VMEM((n, groups, piece, depth), BF16),
+            pltpu.VMEM((n, groups, piece, depth), BF16),
+            pltpu.VMEM((n, groups, piece, depth), BF16),
             pltpu.SemaphoreType.DMA((2, 2, n)),
             pltpu.SemaphoreType.DMA((2, 2, n)),
             pltpu.SemaphoreType.DMA((2, n)),
@@ -418,6 +426,8 @@
             pltpu.SemaphoreType.DMA((groups,)),
             pltpu.SemaphoreType.DMA((n,)),
             pltpu.SemaphoreType.DMA((n,)),
+            pltpu.SemaphoreType.DMA((n, groups)),
+            pltpu.SemaphoreType.DMA((n, groups)),
         ],
         compiler_params=pltpu.CompilerParams(
             collective_id=call, has_side_effects=True, vmem_limit_bytes=VMEM_LIMIT
@@ -469,13 +479,12 @@
         "rkb,sk->srb", x_blocks, row_onehot.astype(jnp.bfloat16), preferred_element_type=jnp.float32
     ).astype(jnp.bfloat16)
     contrib = jnp.einsum("srb,sbn->srn", picked, blocks, preferred_element_type=jnp.float32)
-    placed = jnp.einsum("srn,sc->rcn", contrib, col_onehot, precision=lax.Precision.HIGHEST)
-    placed = placed.reshape(rows, local_ff)
+    placed = jnp.einsum("srn,sc->crn", contrib, col_onehot, precision=lax.Precision.HIGHEST)
     passes = passes_of(shards, rows, local_ff, w_down.shape[1])
     piece = tokens.shape[0] // passes
     depth = w_down.shape[1]
     x_cols = x_cols.reshape(shards, groups, passes, piece, depth)
-    placed = placed.reshape(groups, passes, piece, local_ff)
+    placed = placed.reshape(col_count, groups, passes, piece, side)
     outs, slopes = [], []
     for p in range(passes):
         out, slope = middle(
@@ -486,16 +495,15 @@
             cotangent[p * piece : (p + 1) * piece],
             w_up,
             w_down,
-            placed[:, p].reshape(-1, local_ff),
-        )
-        outs.append(out.reshape(shards, groups, piece, depth))
-        slopes.append(slope.reshape(groups, piece, local_ff))
-    partial_out = jnp.concatenate(outs, axis=2).transpose(1, 0, 2, 3)
-    dpre = jnp.concatenate(slopes, axis=1)
+            placed[:, :, p].reshape(col_count, -1, side),
+        )
+        outs.append(out)
+        slopes.append(slope.reshape(col_count, groups, piece, side))
+    own_out = jnp.concatenate(outs, axis=1)
+    slope_blocks = jnp.concatenate(slopes, axis=2).reshape(col_count, rows, side)
     factor = 1.0 / math.sqrt(rows * shards)
-    slope_blocks = dpre.reshape(rows, col_count, side)
     chosen = jnp.einsum(
-        "rcb,sc->srb",
+        "crb,sc->srb",
         slope_blocks,
         col_onehot.astype(jnp.bfloat16),
         preferred_element_type=jnp.float32,
@@ -503,7 +511,7 @@
     grads = jnp.einsum("srk,srn->skn", picked, chosen, preferred_element_type=jnp.float32)
     grads = grads * factor
     grads = grads.astype(BF16).reshape((shards,) + delta.shape)
-    layer_out, owned_grad = back(shards, groups, 1, partial_out, grads)
+    layer_out, owned_grad = back(shards, groups, 1, own_out, grads)
     new_first = 0.9 * first_moment + 0.1 * owned_grad
     new_second = 0.95 * second_moment + 0.05 * owned_grad * owned_grad
     corrected_first = new_first / (1.0 - 0.9**10)

time: 219 us -> 204 us (0.932); the launches traced: 216 us -> 204 us
  local copies, waits for them, and re-layouts: 15.6 us -> 7.71 us
  Pallas kernels: 188 us -> 185 us
    pallas_call x1, Pallas kernels: 126 us -> 135 us  [middle(): pl.pallas_call(functools.partial(middle_kernel, n), out_shape=(jax.ShapeD...]
    pallas_call x1, Pallas kernels: 25.7 us -> 17.6 us  [back(): pl.pallas_call(functools.partial(back_kernel, n, groups), out_shape=(jax....]
    pallas_call x1, Pallas kernels: 37 us -> 31.9 us  [front(): pl.pallas_call(functools.partial(front_kernel, n), out_shape=(jax.ShapeDt...]
    another operation x2 -> x0, local copies, waits for them, and re-layouts: 4.62 us -> none  [the longest x1 2.76 us: on_device(): placed[:, p].reshape(-1, local_ff)]
    transpose x1 -> x0, local copies, waits for them, and re-layouts: 2.88 us -> none  [on_device(): jnp.einsum('srn,sc->rcn', contrib, col_onehot, precision=lax.Precision.HI...]
    dot_general x0 -> x1, local copies, waits for them, and re-layouts: none -> 2.33 us  [on_device(): jnp.einsum('srn,sc->crn', contrib, col_onehot, precision=lax.Precision.HI...]
where the time goes in v4:
time: 204 us
  Pallas kernels  185 us (91%)
  local copies, waits for them, and re-layouts  7.71 us (4%)
  matrix products  7.66 us (4%)
  other arithmetic  2.69 us (1%)
    pallas_call x1, Pallas kernels, middle(): pl.pallas_call(functools.partial(middle_kernel, n), out_shape=(jax.ShapeD...  135 us
    pallas_call x1, Pallas kernels, front(): pl.pallas_call(functools.partial(front_kernel, n), out_shape=(jax.ShapeDt...  31.9 us
    pallas_call x1, Pallas kernels, back(): pl.pallas_call(functools.partial(back_kernel, n, groups), out_shape=(jax....  17.6 us

profile of v4, /device:TPU:0, one launch (start us, length us, event | category | flops | bytes accessed | tf_op | source)
XLA Modules:
  0.0 203.8 jit_solution(5859660762884193299)
XLA Ops:
  0.6 0.7 dynamic_slice.11
  1.4 0.7 dynamic-slice_convert_fusion
  2.1 1.0 convert_element_type.25.blk_ref
  3.1 0.0 copy-start.1
  3.1 0.9 copy-done.1
  4.0 31.9 %front.1 = (bf16[4,32,4096]{2,1,0:T(8,128)(2,1)S(1)}, bf16[8,4,32,512]{3,2,1,0:T(8,128)(2,1)S(1)}, bf16[8,4,128,128]{3,2,1,0:T(8,128)(2,1)S(1)}) custom-call(bf16[32,4096]{1,0:T(8,128)(2,1)S(1)} %copy-done.1, bf16[4,128,128]{2,1,0:T(8,128)(2,1)S(1)} %convert_element_type.25.blk_ref), custom_call_target="tpu_custom_call" | custom-call | tf_op jit(solution)/shard_map/front/pallas_call | solution.py:134
  35.9 0.0 copy-start.2
  36.0 0.2 copy.20
  36.2 0.7 copy-done.2
  36.9 1.5 convolution_convert_fusion
  38.4 1.9 copy.15
  40.3 0.5 fusion.19
  40.8 3.0 %fusion = f32[28,128,128]{2,0,1:T(8,128)S(1)} fusion(f32[32,128,128]{2,1,0:T(8,128)S(1)} %fusion.19, f32[32]{0:T(128)S(1)} %get-tuple-element.21, s32[32]{0:T(128)S(1)} %get-tuple-element.22), kind=kOutput, calls=%fused_computation.1 | convolution fusion | flops 176162560 | bytes 3932416 | tf_op jit(solution)/shard_map/srn,sc->crn/dot_general | solution.py:482
  43.9 2.3 %copy.14.placed_ref = f32[28,128,128]{2,1,0:T(8,128)} copy(f32[28,128,128]{2,0,1:T(8,128)S(1)} %fusion) | data formatting | bytes 3670016 | tf_op jit(solution)/shard_map/srn,sc->crn/dot_general | solution.py:482
  46.2 135.4 %middle.1 = (bf16[8,32,512]{2,1,0:T(8,128)(2,1)}, bf16[28,128,128]{2,1,0:T(8,128)(2,1)}) custom-call(bf16[1024,512]{1,0:T(8,128)(2,1)} %bitcast.22, bf16[32,4096]{1,0:T(8,128)(2,1)} %cot_ref.1, bf16[512,3584]{1,0:T(8,128)(2,1)} %up_ref.1, bf16[3584,512]{1,0:T(8,128)(2,1)} %down_ref.1, f32[28,128,128]{2,1,0:T(8,128)} %copy.14.placed_ref), custom_call_target="tpu_custom_call" | custom-call | flops 11274289152 | bytes 7340032 | tf_op jit(solution)/shard_map/middle/pallas_call | solution.py:404
  181.6 1.9 fusion.2
  183.4 0.0 copy-start
  183.5 0.0 copy-start.3
  183.5 0.0 copy-start.4
  183.5 0.0 copy-start.5
  183.5 0.8 multiply_convert_fusion
  184.3 0.1 copy-done
  184.4 17.6 %back.1 = (bf16[32,4096]{1,0:T(8,128)(2,1)S(1)}, f32[4,128,128]{2,1,0:T(8,128)S(1)}) custom-call(bf16[8,32,512]{2,1,0:T(8,128)(2,1)S(1)} %copy-done, bf16[8,4,128,128]{3,2,1,0:T(8,128)(2,1)S(1)} %bitcast.19), custom_call_target="tpu_custom_call" | custom-call | tf_op jit(solution)/shard_map/back/pallas_call | solution.py:202
  202.0 0.0 copy-done.3
  202.1 0.0 copy-done.4
  202.1 0.0 copy-done.5
  202.1 1.0 divide_subtract_fusion
  203.0 0.7 copy.28
Async XLA Ops:
  3.1 1.0 copy-start.1
  35.9 1.0 copy-start.2
  183.4 1.0 copy-start
  183.5 18.6 %copy-start.3 = (f32[4,128,128]{2,1,0:T(8,128)S(1)}, f32[4,128,128]{2,1,0:T(8,128)}, u32[]{:S(2)}) copy-start(f32[4,128,128]{2,1,0:T(8,128)} %param.14) | copy-start | bytes 786436
  183.5 18.6 %copy-start.4 = (f32[4,128,128]{2,1,0:T(8,128)S(1)}, f32[4,128,128]{2,1,0:T(8,128)}, u32[]{:S(2)}) copy-start(f32[4,128,128]{2,1,0:T(8,128)} %param.15) | copy-start | bytes 786436
  183.5 18.6 %copy-start.5 = (f32[4,128,128]{2,1,0:T(8,128)S(1)}, f32[4,128,128]{2,1,0:T(8,128)}, u32[]{:S(2)}) copy-start(f32[4,128,128]{2,1,0:T(8,128)} %param.16) | copy-start | bytes 786436
